TPU v7x, 512 devices: a whole 4x8x8 slice. The times are simulated.
512 devices in a mesh: blk: 32 (over z_hi, y), tensor: 16 (over x, z_lo, core).
Axes of the slice: x: 4, y: 8, z: 8 (z_hi: 4, z_lo: 2; z = z_hi * 2 + z_lo), core: 2. Of those that a mesh axis runs over, the one named last changes fastest.
Arguments:
- tokens: bfloat16 [8192, 2560], P('blk'), may hold values from -11 to 11
- doc_ids: int32 [8192], P('blk'), may hold values from 0 to 127, never falling along the last dimension, each value on 1 to 128 neighbouring positions
- qkv_weight: bfloat16 [2560, 3, 4096], P('blk', None, 'tensor'), may hold values from -0.15811388 to 0.15811388
- out_weight: bfloat16 [4096, 2560], P('tensor', 'blk'), may hold values from -0.09375 to 0.09375
- cotangent: bfloat16 [8192, 2560], P('blk'), may hold values from -0.5 to 0.5
Outputs:
- mixed: bfloat16 [8192, 2560], P('blk')
- grad_qkv: float32 [2560, 3, 4096], P('blk', None, 'tensor')
- grad_out: float32 [4096, 2560], P('tensor', 'blk')
Inputs may be any that keep to these rules, and one draw needn't show every extreme that they name: `doc_ids`: never falls along the tokens; a document holds at most half of 256 tokens, and one holds exactly that many.
All inputs are finite; a program needn't handle non-finite values.
Results may differ from a plain program's by a relative error of at most 0.028.
Values may be sent and summed in bfloat16 or wider, within the bound.
A program may use at most 64 MiB of HBM per device.

v0:
```python
import math

import jax
import jax.numpy as jnp
from jax import lax
from jax.sharding import PartitionSpec as P

HD = 128


def shortened(x):

    def short(part):
        return part.astype(jnp.bfloat16) if part.dtype == jnp.float32 else part

    return jax.tree.map(short, x)


def passed_along(x, axis, by):
    length = lax.axis_size(axis)
    return lax.ppermute(x, axis, [(i, (i + by) % length) for i in range(length)])


def rotate_pairs(tensor, positions):
    half_width = tensor.shape[-1] // 2
    exponent = jnp.arange(half_width, dtype=jnp.float32) * (2.0 / tensor.shape[-1])
    frequency = jnp.exp(-math.log(10000.0) * exponent)
    angles = positions[:, None] * frequency[None, :]
    cosine = jnp.cos(angles)[:, None, :]
    sine = jnp.sin(angles)[:, None, :]
    lower = tensor[..., :half_width]
    upper = tensor[..., half_width:]
    return jnp.concatenate([lower * cosine - upper * sine, upper * cosine + lower * sine], axis=-1)


def attention_weights(query_rows, key_rows, doc_ids):
    length = query_rows.shape[0]
    positions = jnp.arange(length, dtype=jnp.float32)
    query_rot = rotate_pairs(query_rows, positions)
    key_rot = rotate_pairs(key_rows, positions)
    scores = jnp.einsum("shd,thd->hst", query_rot, key_rot, precision=lax.Precision.HIGHEST)
    scores = scores / math.sqrt(query_rows.shape[-1])
    order = jnp.arange(length, dtype=jnp.int32)
    allowed = (order[None, :] <= order[:, None]) & (doc_ids[None, :] == doc_ids[:, None])
    scores = jnp.where(allowed[None], scores, -1e30)
    highest = jnp.max(scores, axis=-1, keepdims=True)
    expo_terms = jnp.exp(scores - highest)
    return expo_terms / jnp.sum(expo_terms, axis=-1, keepdims=True)


def forward_context(query_rows, key_rows, value_rows, doc_ids):
    attention = attention_weights(
        query_rows.astype(jnp.float32), key_rows.astype(jnp.float32), doc_ids
    )
    attention = attention.astype(jnp.bfloat16)
    return jnp.einsum("hst,thd->shd", attention, value_rows, preferred_element_type=jnp.float32)


def context_exact(query_rows, key_rows, value_rows, doc_ids):
    attention = attention_weights(query_rows, key_rows, doc_ids)
    return jnp.einsum("hst,thd->shd", attention, value_rows, precision=lax.Precision.HIGHEST)


def take_block(source, block):
    return lax.dynamic_index_in_dim(source, block, 0, keepdims=False)


def take_pair(arrays, block):
    return (take_block(arrays[0], block), take_block(arrays[1], block))


def add_pair(left_pair, right_pair):
    return (left_pair[0] + right_pair[0], left_pair[1] + right_pair[1])


def local(tokens, doc_ids, qkv_weight, out_weight, cotangent):
    length = tokens.shape[0]
    width = tokens.shape[1]
    feature_dev = qkv_weight.shape[2]
    heads_dev = feature_dev // HD
    joined_width = 3 * feature_dev
    weight_piece = lax.all_gather(qkv_weight, "blk", axis=0, tiled=True)
    count = weight_piece.shape[0]
    flat_piece = weight_piece.reshape(count, joined_width)
    joined = jnp.dot(tokens, flat_piece, preferred_element_type=jnp.float32).astype(jnp.bfloat16)
    split = joined.reshape(length, 3, heads_dev, HD)
    query_rows = split[:, 0]
    key_rows = split[:, 1]
    value_rows = split[:, 2]
    context = forward_context(query_rows, key_rows, value_rows, doc_ids).astype(jnp.bfloat16)
    context = context.reshape(length, feature_dev)
    weight_piece = lax.all_gather(out_weight, "blk", axis=1, tiled=True)
    column_block = jnp.dot(context, weight_piece, preferred_element_type=jnp.float32)
    partial_value = column_block
    back_sum = lax.dot_general(
        cotangent, weight_piece, (((1,), (1,)), ((), ())), preferred_element_type=jnp.float32
    )
    partial_value, back_sum = (partial_value, back_sum)
    summed = lax.psum(partial_value.astype(jnp.bfloat16), "tensor").astype(jnp.float32)
    mixed = (tokens.astype(jnp.float32) + summed).astype(jnp.bfloat16)
    back_context = back_sum.astype(jnp.bfloat16)

    def local_context(query_in, key_in, value_in):
        return context_exact(query_in, key_in, value_in, doc_ids)

    unused, pullback = jax.vjp(
        local_context,
        query_rows.astype(jnp.float32),
        key_rows.astype(jnp.float32),
        value_rows.astype(jnp.float32),
    )
    grads = pullback(back_context.astype(jnp.float32).reshape(length, heads_dev, HD))
    grad_joined = jnp.stack(grads, axis=1).astype(jnp.bfloat16).reshape(length, joined_width)
    grad_rows = lax.dot_general(
        tokens, grad_joined, (((0,), (0,)), ((), ())), preferred_element_type=jnp.float32
    )
    grad_cols = lax.dot_general(
        cotangent, context, (((0,), (0,)), ((), ())), preferred_element_type=jnp.float32
    )
    count_blk = lax.axis_size("blk")
    place = lax.axis_index("blk")
    row_count = width // count_blk
    row_blocks = grad_rows.reshape(count_blk, row_count, joined_width)
    col_blocks = grad_cols.reshape(count_blk, row_count, feature_dev)
    blocks = (row_blocks, col_blocks)
    starting = take_pair(blocks, (place - 1) % count_blk)

    def hop_single(hop_index, running):
        received = jax.tree.map(
            lambda part, own: part.astype(own.dtype),
            passed_along(shortened(running), "blk", 1),
            running,
        )
        return add_pair(received, take_pair(blocks, (place - 2 - hop_index) % count_blk))

    total_rows, total_cols = lax.fori_loop(0, count_blk - 1, hop_single, starting)
    grad_qkv = total_rows.reshape(row_count, 3, feature_dev)
    grad_out = total_cols.T
    return (mixed, grad_qkv, grad_out)


def solution(mesh):
    placed = (
        P("blk", None),
        P("blk"),
        P("blk", None, "tensor"),
        P("tensor", "blk"),
        P("blk", None),
    )
    return jax.shard_map(
        local,
        mesh=mesh,
        in_specs=placed,
        out_specs=(P("blk", None), P("blk", None, "tensor"), P("tensor", "blk")),
        check_vma=False,
    )
```

profile of v0, /device:TPU:6, one launch (start us, length us, event | category | flops | bytes accessed | tf_op | source)
XLA Modules:
  0.0 713.7 jit_solution(17127050844784503828)
XLA Ops:
  10.1 90.2 %all-gather.5.cloned.1.call-done = bf16[256,2560]{0,1:T(8,128)(2,1)} async-done(((bf16[256,80]{0,1:T(8,128)(2,1)}), bf16[256,2560]{0,1:T(8,128)(2,1)}) %all-gather.5.cloned.1.call-update) | async-done | bytes 1310736 | tf_op jit(solution)/shard_map/all_gather | solution.py:92
  103.0 97.7 %all-gather.3.cloned.1.call-done = bf16[2560,3,256]{2,0,1:T(8,128)(2,1)} async-done(((bf16[80,3,256]{2,0,1:T(8,128)(2,1)}), bf16[2560,3,256]{2,0,1:T(8,128)(2,1)}) %all-gather.3.cloned.1.call-update) | async-done | bytes 3932176 | tf_op jit(solution)/shard_map/all_gather | solution.py:82
  228.8 9.1 %copy.58 = f32[2560,768]{1,0:T(8,128)} copy(f32[2560,768]{0,1:T(8,128)} %convolution_bitcast_fusion) | data formatting | bytes 15728640 | tf_op jit(solution)/shard_map/dot_general | solution.py:114
  243.0 460.7 %while.17 = (s32[]{:T(128)}, f32[80,768]{1,0:T(8,128)S(1)}, f32[80,256]{1,0:T(8,128)S(1)}, s32[]{:T(128)}, f32[32,80,768]{2,1,0:T(8,128)}, /*index=5*/f32[32,80,...) while((s32[]{:T(128)}, f32[80,768]{1,0:T(8,128)S(1)}, f32[80,256]{1,0:T(8,128)S(1)}, s32[]{:T(128)}, ...), condition=%wide.region_7.8_spmd, body=%wide.region_6.7_spmd.sunk | while | flops 245777 | bytes 1966424 | solution.py:136
  277.2 6.6 collective-permute-done.1
  305.8 6.7 collective-permute-done.1
  320.9 6.7 collective-permute-done.1
  378.7 6.6 collective-permute-done.1
  394.5 7.3 %collective-permute-done.1 = bf16[80,256]{1,0:T(8,128)(2,1)S(1)} collective-permute-done((bf16[80,256]{1,0:T(8,128)(2,1)S(1)}, bf16[80,256]{1,0:T(8,128)(2,1)S(1)}, u32[]{:S(2)}, u32[]{:S(2)}) %collective-permute-start.1) | collective-permute-done | bytes 40992 | tf_op jit(solution)/shard_map/while/body/eval_jaxpr/ppermute | solution.py:21
  425.5 6.8 collective-permute-done.1
  439.8 8.1 %collective-permute-done.1 = bf16[80,256]{1,0:T(8,128)(2,1)S(1)} collective-permute-done((bf16[80,256]{1,0:T(8,128)(2,1)S(1)}, bf16[80,256]{1,0:T(8,128)(2,1)S(1)}, u32[]{:S(2)}, u32[]{:S(2)}) %collective-permute-start.1) | collective-permute-done | bytes 40992 | tf_op jit(solution)/shard_map/while/body/eval_jaxpr/ppermute | solution.py:21
  454.7 7.8 %collective-permute-done.1 = bf16[80,256]{1,0:T(8,128)(2,1)S(1)} collective-permute-done((bf16[80,256]{1,0:T(8,128)(2,1)S(1)}, bf16[80,256]{1,0:T(8,128)(2,1)S(1)}, u32[]{:S(2)}, u32[]{:S(2)}) %collective-permute-start.1) | collective-permute-done | bytes 40992 | tf_op jit(solution)/shard_map/while/body/eval_jaxpr/ppermute | solution.py:21
  469.6 6.8 collective-permute-done.1
  513.2 6.6 collective-permute-done.1
  528.5 6.7 collective-permute-done.1
  544.9 7.2 %collective-permute-done.1 = bf16[80,256]{1,0:T(8,128)(2,1)S(1)} collective-permute-done((bf16[80,256]{1,0:T(8,128)(2,1)S(1)}, bf16[80,256]{1,0:T(8,128)(2,1)S(1)}, u32[]{:S(2)}, u32[]{:S(2)}) %collective-permute-start.1) | collective-permute-done | bytes 40992 | tf_op jit(solution)/shard_map/while/body/eval_jaxpr/ppermute | solution.py:21
  562.0 6.7 collective-permute-done.1
  578.2 7.4 %collective-permute-done.1 = bf16[80,256]{1,0:T(8,128)(2,1)S(1)} collective-permute-done((bf16[80,256]{1,0:T(8,128)(2,1)S(1)}, bf16[80,256]{1,0:T(8,128)(2,1)S(1)}, u32[]{:S(2)}, u32[]{:S(2)}) %collective-permute-start.1) | collective-permute-done | bytes 40992 | tf_op jit(solution)/shard_map/while/body/eval_jaxpr/ppermute | solution.py:21
  593.4 6.8 collective-permute-done.1
  607.8 6.6 collective-permute-done.1
  622.2 6.6 collective-permute-done.1
  650.9 6.6 collective-permute-done.1
  665.4 6.6 collective-permute-done.1
  679.8 6.6 collective-permute-done.1
  (282 shorter events, 362.5 us)
Async XLA Ops:
  7.2 93.2 %all-gather.5.cloned.1.call-start = ((), (), s32[]{:S(2)}) async-start(), calls=%async_computation.1 | async-start | bytes 1351680 | tf_op jit(solution)/shard_map/all_gather | solution.py:92
  7.9 192.8 %all-gather.3.cloned.1.call-start = ((), (), s32[]{:S(2)}) async-start(), calls=%async_computation | async-start | bytes 4055040 | tf_op jit(solution)/shard_map/all_gather | solution.py:82
  8.7 695.8 %all-reduce.6.cloned.1.call-start = ((), (), s32[]{:S(2)}) async-start(), calls=%async_computation.2 | async-start | bytes 2621440 | tf_op jit(solution)/shard_map/psum | solution.py:99
  243.1 11.9 %collective-permute-start.1 = (bf16[80,256]{1,0:T(8,128)(2,1)S(1)}, bf16[80,256]{1,0:T(8,128)(2,1)S(1)}, u32[]{:S(2)}, u32[]{:S(2)}) collective-permute-start(bf16[80,256]{1,0:T(8,128)(2,1)S(1)} %convert_element_type.127), channel_id=1, source_target_pairs={{0,16},{16,32},{32,48},{48,64},{64,80},{80,96},{96,112},{112,128},... | collective-permute-start | bytes 122888 | tf_op jit(solution)/shard_map/while/body/eval_jaxpr/ppermute | solution.py:21
  245.6 12.6 %collective-permute-start = (bf16[80,768]{1,0:T(8,128)(2,1)S(1)}, bf16[80,768]{1,0:T(8,128)(2,1)S(1)}, u32[]{:S(2)}, u32[]{:S(2)}) collective-permute-start(bf16[80,768]{1,0:T(8,128)(2,1)S(1)} %convert_element_type.126), channel_id=1, source_target_pairs={{0,16},{16,32},{32,48},{48,64},{64,80},{80,96},{96,112},{112,128},... | collective-permute-start | bytes 368648 | tf_op jit(solution)/shard_map/while/body/eval_jaxpr/ppermute | solution.py:21
  289.5 11.4 %collective-permute-start = (bf16[80,768]{1,0:T(8,128)(2,1)S(1)}, bf16[80,768]{1,0:T(8,128)(2,1)S(1)}, u32[]{:S(2)}, u32[]{:S(2)}) collective-permute-start(bf16[80,768]{1,0:T(8,128)(2,1)S(1)} %convert_element_type.126), channel_id=1, source_target_pairs={{0,16},{16,32},{32,48},{48,64},{64,80},{80,96},{96,112},{112,128},... | collective-permute-start | bytes 368648 | tf_op jit(solution)/shard_map/while/body/eval_jaxpr/ppermute | solution.py:21
  303.9 12.1 %collective-permute-start = (bf16[80,768]{1,0:T(8,128)(2,1)S(1)}, bf16[80,768]{1,0:T(8,128)(2,1)S(1)}, u32[]{:S(2)}, u32[]{:S(2)}) collective-permute-start(bf16[80,768]{1,0:T(8,128)(2,1)S(1)} %convert_element_type.126), channel_id=1, source_target_pairs={{0,16},{16,32},{32,48},{48,64},{64,80},{80,96},{96,112},{112,128},... | collective-permute-start | bytes 368648 | tf_op jit(solution)/shard_map/while/body/eval_jaxpr/ppermute | solution.py:21
  347.1 11.5 %collective-permute-start = (bf16[80,768]{1,0:T(8,128)(2,1)S(1)}, bf16[80,768]{1,0:T(8,128)(2,1)S(1)}, u32[]{:S(2)}, u32[]{:S(2)}) collective-permute-start(bf16[80,768]{1,0:T(8,128)(2,1)S(1)} %convert_element_type.126), channel_id=1, source_target_pairs={{0,16},{16,32},{32,48},{48,64},{64,80},{80,96},{96,112},{112,128},... | collective-permute-start | bytes 368648 | tf_op jit(solution)/shard_map/while/body/eval_jaxpr/ppermute | solution.py:21
  361.6 12.2 %collective-permute-start = (bf16[80,768]{1,0:T(8,128)(2,1)S(1)}, bf16[80,768]{1,0:T(8,128)(2,1)S(1)}, u32[]{:S(2)}, u32[]{:S(2)}) collective-permute-start(bf16[80,768]{1,0:T(8,128)(2,1)S(1)} %convert_element_type.126), channel_id=1, source_target_pairs={{0,16},{16,32},{32,48},{48,64},{64,80},{80,96},{96,112},{112,128},... | collective-permute-start | bytes 368648 | tf_op jit(solution)/shard_map/while/body/eval_jaxpr/ppermute | solution.py:21
  376.8 12.8 %collective-permute-start = (bf16[80,768]{1,0:T(8,128)(2,1)S(1)}, bf16[80,768]{1,0:T(8,128)(2,1)S(1)}, u32[]{:S(2)}, u32[]{:S(2)}) collective-permute-start(bf16[80,768]{1,0:T(8,128)(2,1)S(1)} %convert_element_type.126), channel_id=1, source_target_pairs={{0,16},{16,32},{32,48},{48,64},{64,80},{80,96},{96,112},{112,128},... | collective-permute-start | bytes 368648 | tf_op jit(solution)/shard_map/while/body/eval_jaxpr/ppermute | solution.py:21
  392.5 13.7 %collective-permute-start = (bf16[80,768]{1,0:T(8,128)(2,1)S(1)}, bf16[80,768]{1,0:T(8,128)(2,1)S(1)}, u32[]{:S(2)}, u32[]{:S(2)}) collective-permute-start(bf16[80,768]{1,0:T(8,128)(2,1)S(1)} %convert_element_type.126), channel_id=1, source_target_pairs={{0,16},{16,32},{32,48},{48,64},{64,80},{80,96},{96,112},{112,128},... | collective-permute-start | bytes 368648 | tf_op jit(solution)/shard_map/while/body/eval_jaxpr/ppermute | solution.py:21
  435.9 12.0 %collective-permute-start.1 = (bf16[80,256]{1,0:T(8,128)(2,1)S(1)}, bf16[80,256]{1,0:T(8,128)(2,1)S(1)}, u32[]{:S(2)}, u32[]{:S(2)}) collective-permute-start(bf16[80,256]{1,0:T(8,128)(2,1)S(1)} %convert_element_type.127), channel_id=1, source_target_pairs={{0,16},{16,32},{32,48},{48,64},{64,80},{80,96},{96,112},{112,128},... | collective-permute-start | bytes 122888 | tf_op jit(solution)/shard_map/while/body/eval_jaxpr/ppermute | solution.py:21
  437.9 12.0 %collective-permute-start = (bf16[80,768]{1,0:T(8,128)(2,1)S(1)}, bf16[80,768]{1,0:T(8,128)(2,1)S(1)}, u32[]{:S(2)}, u32[]{:S(2)}) collective-permute-start(bf16[80,768]{1,0:T(8,128)(2,1)S(1)} %convert_element_type.126), channel_id=1, source_target_pairs={{0,16},{16,32},{32,48},{48,64},{64,80},{80,96},{96,112},{112,128},... | collective-permute-start | bytes 368648 | tf_op jit(solution)/shard_map/while/body/eval_jaxpr/ppermute | solution.py:21
  450.8 11.7 %collective-permute-start.1 = (bf16[80,256]{1,0:T(8,128)(2,1)S(1)}, bf16[80,256]{1,0:T(8,128)(2,1)S(1)}, u32[]{:S(2)}, u32[]{:S(2)}) collective-permute-start(bf16[80,256]{1,0:T(8,128)(2,1)S(1)} %convert_element_type.127), channel_id=1, source_target_pairs={{0,16},{16,32},{32,48},{48,64},{64,80},{80,96},{96,112},{112,128},... | collective-permute-start | bytes 122888 | tf_op jit(solution)/shard_map/while/body/eval_jaxpr/ppermute | solution.py:21
  452.8 11.9 %collective-permute-start = (bf16[80,768]{1,0:T(8,128)(2,1)S(1)}, bf16[80,768]{1,0:T(8,128)(2,1)S(1)}, u32[]{:S(2)}, u32[]{:S(2)}) collective-permute-start(bf16[80,768]{1,0:T(8,128)(2,1)S(1)} %convert_element_type.126), channel_id=1, source_target_pairs={{0,16},{16,32},{32,48},{48,64},{64,80},{80,96},{96,112},{112,128},... | collective-permute-start | bytes 368648 | tf_op jit(solution)/shard_map/while/body/eval_jaxpr/ppermute | solution.py:21
  467.6 11.4 %collective-permute-start = (bf16[80,768]{1,0:T(8,128)(2,1)S(1)}, bf16[80,768]{1,0:T(8,128)(2,1)S(1)}, u32[]{:S(2)}, u32[]{:S(2)}) collective-permute-start(bf16[80,768]{1,0:T(8,128)(2,1)S(1)} %convert_element_type.126), channel_id=1, source_target_pairs={{0,16},{16,32},{32,48},{48,64},{64,80},{80,96},{96,112},{112,128},... | collective-permute-start | bytes 368648 | tf_op jit(solution)/shard_map/while/body/eval_jaxpr/ppermute | solution.py:21
  496.3 11.9 %collective-permute-start = (bf16[80,768]{1,0:T(8,128)(2,1)S(1)}, bf16[80,768]{1,0:T(8,128)(2,1)S(1)}, u32[]{:S(2)}, u32[]{:S(2)}) collective-permute-start(bf16[80,768]{1,0:T(8,128)(2,1)S(1)} %convert_element_type.126), channel_id=1, source_target_pairs={{0,16},{16,32},{32,48},{48,64},{64,80},{80,96},{96,112},{112,128},... | collective-permute-start | bytes 368648 | tf_op jit(solution)/shard_map/while/body/eval_jaxpr/ppermute | solution.py:21
  511.2 12.3 %collective-permute-start = (bf16[80,768]{1,0:T(8,128)(2,1)S(1)}, bf16[80,768]{1,0:T(8,128)(2,1)S(1)}, u32[]{:S(2)}, u32[]{:S(2)}) collective-permute-start(bf16[80,768]{1,0:T(8,128)(2,1)S(1)} %convert_element_type.126), channel_id=1, source_target_pairs={{0,16},{16,32},{32,48},{48,64},{64,80},{80,96},{96,112},{112,128},... | collective-permute-start | bytes 368648 | tf_op jit(solution)/shard_map/while/body/eval_jaxpr/ppermute | solution.py:21
  526.5 13.4 %collective-permute-start = (bf16[80,768]{1,0:T(8,128)(2,1)S(1)}, bf16[80,768]{1,0:T(8,128)(2,1)S(1)}, u32[]{:S(2)}, u32[]{:S(2)}) collective-permute-start(bf16[80,768]{1,0:T(8,128)(2,1)S(1)} %convert_element_type.126), channel_id=1, source_target_pairs={{0,16},{16,32},{32,48},{48,64},{64,80},{80,96},{96,112},{112,128},... | collective-permute-start | bytes 368648 | tf_op jit(solution)/shard_map/while/body/eval_jaxpr/ppermute | solution.py:21
  542.9 14.1 %collective-permute-start = (bf16[80,768]{1,0:T(8,128)(2,1)S(1)}, bf16[80,768]{1,0:T(8,128)(2,1)S(1)}, u32[]{:S(2)}, u32[]{:S(2)}) collective-permute-start(bf16[80,768]{1,0:T(8,128)(2,1)S(1)} %convert_element_type.126), channel_id=1, source_target_pairs={{0,16},{16,32},{32,48},{48,64},{64,80},{80,96},{96,112},{112,128},... | collective-permute-start | bytes 368648 | tf_op jit(solution)/shard_map/while/body/eval_jaxpr/ppermute | solution.py:21
  560.0 13.2 %collective-permute-start = (bf16[80,768]{1,0:T(8,128)(2,1)S(1)}, bf16[80,768]{1,0:T(8,128)(2,1)S(1)}, u32[]{:S(2)}, u32[]{:S(2)}) collective-permute-start(bf16[80,768]{1,0:T(8,128)(2,1)S(1)} %convert_element_type.126), channel_id=1, source_target_pairs={{0,16},{16,32},{32,48},{48,64},{64,80},{80,96},{96,112},{112,128},... | collective-permute-start | bytes 368648 | tf_op jit(solution)/shard_map/while/body/eval_jaxpr/ppermute | solution.py:21
  576.2 12.3 %collective-permute-start = (bf16[80,768]{1,0:T(8,128)(2,1)S(1)}, bf16[80,768]{1,0:T(8,128)(2,1)S(1)}, u32[]{:S(2)}, u32[]{:S(2)}) collective-permute-start(bf16[80,768]{1,0:T(8,128)(2,1)S(1)} %convert_element_type.126), channel_id=1, source_target_pairs={{0,16},{16,32},{32,48},{48,64},{64,80},{80,96},{96,112},{112,128},... | collective-permute-start | bytes 368648 | tf_op jit(solution)/shard_map/while/body/eval_jaxpr/ppermute | solution.py:21
  591.4 11.5 %collective-permute-start = (bf16[80,768]{1,0:T(8,128)(2,1)S(1)}, bf16[80,768]{1,0:T(8,128)(2,1)S(1)}, u32[]{:S(2)}, u32[]{:S(2)}) collective-permute-start(bf16[80,768]{1,0:T(8,128)(2,1)S(1)} %convert_element_type.126), channel_id=1, source_target_pairs={{0,16},{16,32},{32,48},{48,64},{64,80},{80,96},{96,112},{112,128},... | collective-permute-start | bytes 368648 | tf_op jit(solution)/shard_map/while/body/eval_jaxpr/ppermute | solution.py:21
  648.9 11.5 %collective-permute-start = (bf16[80,768]{1,0:T(8,128)(2,1)S(1)}, bf16[80,768]{1,0:T(8,128)(2,1)S(1)}, u32[]{:S(2)}, u32[]{:S(2)}) collective-permute-start(bf16[80,768]{1,0:T(8,128)(2,1)S(1)} %convert_element_type.126), channel_id=1, source_target_pairs={{0,16},{16,32},{32,48},{48,64},{64,80},{80,96},{96,112},{112,128},... | collective-permute-start | bytes 368648 | tf_op jit(solution)/shard_map/while/body/eval_jaxpr/ppermute | solution.py:21
  (47 other events, 646.0 us)
Sparse Core Ops, SparseCore 0:
  11.2 89.1 all-gather.4
  103.5 97.1 all-gather.2
  223.5 131.8 all-reduce.5
where the time goes:
time: 720 us; the launch traced here: 714 us
  waiting for transfers between devices  467 us (65%)
  starting transfers between devices  122 us (17%)
  other arithmetic  64.8 us (9%)
  local copies, waits for them, and re-layouts  24.5 us (3%)
  matrix products  19 us (3%)
  between operations  13.9 us (2%)
    ppermute x62, waiting for transfers between devices, passed_along(): lax.ppermute(x, axis, [(i, (i + by) % length) for i in range(length)])  278 us
    ppermute x62, starting transfers between devices, passed_along(): lax.ppermute(x, axis, [(i, (i + by) % length) for i in range(length)])  122 us
    all_gather x1, waiting for transfers between devices, local(): weight_piece = lax.all_gather(qkv_weight, 'blk', axis=0, tiled=True)  97.7 us
    all_gather x1, waiting for transfers between devices, local(): weight_piece = lax.all_gather(out_weight, 'blk', axis=1, tiled=True)  90.2 us
    add x62, other arithmetic, add_pair(): return (left_pair[0] + right_pair[0], left_pair[1] + right_pair[1])  57.9 us
  transfers between devices with their start and end apart: 65, of which 64 were waited for; matrix products, arithmetic and copies ran while one was open for 12% of the time, Pallas kernels for 0%

commit v1 on v0

v1 whole, which is shorter than its diff:
```python
import math

import jax
import jax.numpy as jnp
import numpy as np
from jax import lax
from jax.experimental import pallas as pl
from jax.experimental.pallas import tpu as pltpu
from jax.sharding import PartitionSpec as P

HD = 128
NZ, NY = 4, 8
NX, NL, NC = 4, 2, 2
F32 = jnp.float32
BF16 = jnp.bfloat16
HIGHEST = lax.Precision.HIGHEST
NT = (((1,), (1,)), ((), ()))


def dot(a, b):
    return jnp.dot(a, b, preferred_element_type=F32)


def dot_nt(a, b):
    return lax.dot_general(a, b, NT, preferred_element_type=F32)


def turned(x, cosine, sine):
    half = x.shape[1] // 2
    swapped = jnp.concatenate([x[:, half:], x[:, :half]], axis=1)
    return x * cosine + swapped * sine


def kernel(
    tokens_hbm, cot_hbm, wq_in, wo_in, doc_col, doc_row, cos_in, sin_in,
    mixed_out, gq_out, go_out,
    tok, cot, tok_t, cot_t, wq, wo, joined, ctx, back, probs, q_rot, k_rot, grad_j,
    grad_q, grad_o, sq, rq, so, ro, zsq, zrq, zso, zro,
    part, part_c, sum_c, recv_x, sum_x, recv_l, mixed,
    load_sem, ag_ss, ag_rs, agz_ss, agz_rs, rs_ss, rs_rs, rsz_ss, rsz_rs, mx_ss, mx_rs,
):
    blk = lax.axis_index("blk")
    ten = lax.axis_index("tensor")
    zh, y = blk // NY, blk % NY
    x, rest = ten // (NL * NC), ten % (NL * NC)
    lo, core = rest // NC, rest % NC
    rows = wq_in.shape[0]
    length = tok.shape[0]

    def at_z(k):
        return (((zh + k) % NZ) * NY + y, ten)

    def at_y(step):
        return (zh * NY + (y + step + NY) % NY, ten)

    def at_x(k):
        return (blk, ((x + k) % NX) * (NL * NC) + rest)

    up, down = at_y(1), at_y(-1)
    core_peer = (blk, ten + 1 - 2 * core)
    lo_peer = (blk, ten + NC - 2 * NC * lo)

    load_tok = pltpu.make_async_copy(tokens_hbm, tok, load_sem.at[0])
    load_cot = pltpu.make_async_copy(cot_hbm, cot, load_sem.at[1])
    load_tok.start()
    load_cot.start()

    barrier = pltpu.get_barrier_semaphore()
    peers = [at_z(k) for k in (1, 2, 3)] + [up, down, core_peer, lo_peer] + [at_x(k) for k in (1, 2, 3)]
    for peer in peers:
        pl.semaphore_signal(barrier, inc=1, device_id=peer, device_id_type=pl.DeviceIdType.MESH)

    def row_at(z, yy):
        return pl.ds(pl.multiple_of((z * NY + yy) * rows, 16), rows)

    mine = row_at(zh, y)
    wq[mine, :] = wq_in[...]
    wo[mine, :] = wo_in[...]
    pl.semaphore_wait(barrier, len(peers))

    def remote(src, dst, ss, rs, peer):
        return pltpu.make_async_remote_copy(
            src_ref=src, dst_ref=dst, send_sem=ss, recv_sem=rs,
            device_id=peer, device_id_type=pl.DeviceIdType.MESH,
        )

    gathered = (wq, wo)

    def ag_z(p, k):
        w = gathered[p]
        return remote(w.at[mine, :], w.at[mine, :], agz_ss.at[p, k], agz_rs.at[p, k], at_z(k))

    def ag_z_got(p, k):
        w = gathered[p]
        here = row_at((zh - k + NZ) % NZ, y)
        return remote(w.at[here, :], w.at[here, :], agz_ss.at[p, k], agz_rs.at[p, k], at_z(k))

    def ag_y(p, way, s, j, got):
        w = gathered[p]
        sign = 1 if way == 0 else -1
        off = s + 1 if got else s
        here = row_at((zh - j + NZ) % NZ, (y - sign * off + 2 * NY) % NY)
        return remote(
            w.at[here, :], w.at[here, :], ag_ss.at[p, way, s, j], ag_rs.at[p, way, s, j],
            up if way == 0 else down,
        )

    def long_js(way):
        return (0, 2) if way == 0 else (1, 3)

    def ag_first(p):
        for k in (1, 2, 3):
            ag_z(p, k).start()

        for way in (0, 1):
            ag_y(p, way, 0, 0, False).start()

        def body(j, c):
            ag_z_got(p, j).wait_recv()
            for way in (0, 1):
                ag_y(p, way, 0, j, False).start()
            return c

        lax.fori_loop(1, NZ, body, 0)

    def ag_mid(p, s):
        def body(j, c):
            for way in (0, 1):
                ag_y(p, way, s - 1, j, True).wait_recv()
                ag_y(p, way, s, j, False).start()
            return c

        lax.fori_loop(0, NZ, body, 0)

    def ag_last(p):
        for j in range(NZ):
            for way in (0, 1):
                ag_y(p, way, 2, j, True).wait_recv()
                if j in long_js(way):
                    ag_y(p, way, 3, j, False).start()

    def ag_end(p):
        for j in range(NZ):
            for way in (0, 1):
                if j in long_js(way):
                    ag_y(p, way, 3, j, True).wait_recv()

    def ag_drain(p):
        for k in (1, 2, 3):
            ag_z(p, k).wait_send()

        def body(j, c):
            for way in (0, 1):
                for s in range(3):
                    ag_y(p, way, s, j, False).wait_send()
            return c

        lax.fori_loop(0, NZ, body, 0)
        for way in (0, 1):
            for j in long_js(way):
                ag_y(p, way, 3, j, False).wait_send()

    ag_first(0)
    load_tok.wait()
    load_cot.wait()

    def flip(i, c):
        cols = pl.ds(pl.multiple_of(i * 256, 256), 256)
        tok_t[cols, :] = tok[:, cols].T
        cot_t[cols, :] = cot[:, cols].T
        return c

    ag_mid(0, 1)
    lax.fori_loop(0, tok.shape[1] // 256, flip, 0)
    ag_mid(0, 2)
    ag_last(0)
    ag_first(1)
    ag_end(0)

    cosine, sine = cos_in[...], sin_in[...]
    scale = 1.0 / math.sqrt(HD)

    def project():
        joined[...] = dot(tok[...], wq[...]).astype(BF16)

    def attend(h):
        cols = slice(h * HD, (h + 1) * HD)
        width = 2 * HD
        qr = turned(joined[:, h * HD:(h + 1) * HD].astype(F32), cosine, sine)
        kr = turned(joined[:, width + h * HD:width + (h + 1) * HD].astype(F32), cosine, sine)
        q_rot[h] = qr
        k_rot[h] = kr
        scores = lax.dot_general(qr, kr, NT, precision=HIGHEST, preferred_element_type=F32) * scale
        row = lax.broadcasted_iota(jnp.int32, (length, length), 0)
        col = lax.broadcasted_iota(jnp.int32, (length, length), 1)
        allowed = (col <= row) & (doc_row[...] == doc_col[...])
        scores = jnp.where(allowed, scores, -1e30)
        expo = jnp.exp(scores - jnp.max(scores, axis=1, keepdims=True))
        p = expo / jnp.sum(expo, axis=1, keepdims=True)
        probs[h] = p
        values = joined[:, 2 * width + h * HD:2 * width + (h + 1) * HD]
        ctx[:, cols] = dot(p.astype(BF16), values).astype(BF16)

    def retreat(h):
        width = 2 * HD
        p = probs[h]
        d_out = back[:, h * HD:(h + 1) * HD]
        values = joined[:, 2 * width + h * HD:2 * width + (h + 1) * HD]
        d_val = jnp.dot(p.T, d_out.astype(F32), precision=HIGHEST, preferred_element_type=F32)
        d_p = dot_nt(d_out, values)
        d_s = p * (d_p - jnp.sum(p * d_p, axis=1, keepdims=True)) * scale
        d_q = jnp.dot(d_s, k_rot[h], precision=HIGHEST, preferred_element_type=F32)
        d_k = jnp.dot(d_s.T, q_rot[h], precision=HIGHEST, preferred_element_type=F32)
        grad_j[:, h * HD:(h + 1) * HD] = turned(d_q, cosine, -sine).astype(BF16)
        grad_j[:, width + h * HD:width + (h + 1) * HD] = turned(d_k, cosine, -sine).astype(BF16)
        grad_j[:, 2 * width + h * HD:2 * width + (h + 1) * HD] = d_val.astype(BF16)

    project()
    ag_mid(1, 1)
    attend(0)
    ag_mid(1, 2)
    attend(1)
    ag_last(1)

    grads, sends, recvs = (grad_q, grad_o), (sq, so), (rq, ro)
    z_sends, z_recvs = (zsq, zso), (zrq, zro)

    def rs_y(p, way, d, j):
        return remote(
            sends[p].at[way, d - 1, j], recvs[p].at[way, d - 1, j],
            rs_ss.at[p, way, d - 1, j], rs_rs.at[p, way, d - 1, j],
            up if way == 0 else down,
        )

    def rs_own(p, way, d, j):
        sign = 1 if way == 0 else -1
        return grads[p][row_at((zh - j + NZ) % NZ, (y + sign * d + NY) % NY), :]

    def rs_far(p):
        for way in (0, 1):
            for j in long_js(way):
                sends[p][way, 3, j] = rs_own(p, way, 4, j).astype(BF16)
                rs_y(p, way, 4, j).start()

    def rs_three(p):
        for j in (1, 2, 3, 0):
            for way in (0, 1):
                own = rs_own(p, way, 3, j)
                if j in long_js(way):
                    rs_y(p, way, 4, j).wait_recv()
                    own = own + recvs[p][way, 3, j].astype(F32)
                sends[p][way, 2, j] = own.astype(BF16)
                rs_y(p, way, 3, j).start()

    def rs_near(p, d):
        def body(i, c):
            j = (i + 1) % NZ
            for way in (0, 1):
                rs_y(p, way, d + 1, j).wait_recv()
                own = rs_own(p, way, d, j) + recvs[p][way, d, j].astype(F32)
                sends[p][way, d - 1, j] = own.astype(BF16)
                rs_y(p, way, d, j).start()
            return c

        lax.fori_loop(0, NZ, body, 0)

    def rs_z(p, j):
        return remote(
            z_sends[p].at[j], z_recvs[p].at[j], rsz_ss.at[p, j], rsz_rs.at[p, j], at_z(NZ - j)
        )

    def rs_here(p, j):
        for way in (0, 1):
            rs_y(p, way, 1, j).wait_recv()
        own = grads[p][row_at((zh - j + NZ) % NZ, y), :]
        return own + recvs[p][0, 0, j].astype(F32) + recvs[p][1, 0, j].astype(F32)

    def rs_out(p):
        def body(j, c):
            z_sends[p][j] = rs_here(p, j).astype(BF16)
            rs_z(p, j).start()
            return c

        lax.fori_loop(1, NZ, body, 0)

    def rs_end(p, out):
        total = rs_here(p, 0)
        for j in (1, 2, 3):
            rs_z(p, j).wait_recv()
            total = total + z_recvs[p][j].astype(F32)
        out[...] = total

    def rs_drain(p):
        for j in (1, 2, 3):
            rs_z(p, j).wait_send()

        def body(j, c):
            for way in (0, 1):
                for d in (1, 2, 3):
                    rs_y(p, way, d, j).wait_send()
            return c

        lax.fori_loop(0, NZ, body, 0)
        for way in (0, 1):
            for j in long_js(way):
                rs_y(p, way, 4, j).wait_send()

    half = length // NC
    quarter = half // NX
    eighth = quarter // NL
    half_at = pl.ds(pl.multiple_of(core * half, 16), half)
    quarter_at = pl.ds(pl.multiple_of(core * half + x * quarter, 16), quarter)
    eighth_at = pl.ds(pl.multiple_of(core * half + x * quarter + lo * eighth, 16), eighth)

    def mx_core():
        away = pl.ds(pl.multiple_of((1 - core) * half, 16), half)
        return remote(part.at[away, :], part_c, mx_ss.at[0], mx_rs.at[0], core_peer)

    def mx_x(k):
        away = pl.ds(pl.multiple_of(((x + k) % NX) * quarter, 16), quarter)
        return remote(sum_c.at[away, :], recv_x.at[k - 1], mx_ss.at[k], mx_rs.at[k], at_x(k))

    def mx_lo():
        away = pl.ds(pl.multiple_of((1 - lo) * eighth, 16), eighth)
        return remote(sum_x.at[away, :], recv_l, mx_ss.at[4], mx_rs.at[4], lo_peer)

    def back_lo(got=False):
        at = eighth_at
        if got:
            at = pl.ds(pl.multiple_of(core * half + x * quarter + (1 - lo) * eighth, 16), eighth)
        return remote(mixed.at[at, :], mixed.at[at, :], mx_ss.at[5], mx_rs.at[5], lo_peer)

    def back_x(k, got=False):
        at = quarter_at
        if got:
            at = pl.ds(pl.multiple_of(core * half + ((x - k + NX) % NX) * quarter, 16), quarter)
        return remote(mixed.at[at, :], mixed.at[at, :], mx_ss.at[5 + k], mx_rs.at[5 + k], at_x(k))

    def back_core(got=False):
        at = half_at
        if got:
            at = pl.ds(pl.multiple_of((1 - core) * half, 16), half)
        return remote(mixed.at[at, :], mixed.at[at, :], mx_ss.at[9], mx_rs.at[9], core_peer)

    def stage_x():
        mx_core().wait_recv()

        def body(i, c):
            r = pl.ds(pl.multiple_of(i * 16, 16), 16)
            there = pl.ds(pl.multiple_of(core * half + i * 16, 16), 16)
            sum_c[r, :] = (part[there, :].astype(F32) + part_c[r, :].astype(F32)).astype(BF16)
            return c

        lax.fori_loop(0, half // 16, body, 0)
        for k in (1, 2, 3):
            mx_x(k).start()

    def stage_lo():
        total = sum_c[pl.ds(pl.multiple_of(x * quarter, 16), quarter), :].astype(F32)
        for k in (1, 2, 3):
            mx_x(k).wait_recv()
            total = total + recv_x[k - 1].astype(F32)
        sum_x[...] = total.astype(BF16)
        mx_lo().start()

    def stage_back():
        mx_lo().wait_recv()
        own = sum_x[pl.ds(pl.multiple_of(lo * eighth, 16), eighth), :].astype(F32)
        total = tok[eighth_at, :].astype(F32) + (own + recv_l[...].astype(F32))
        mixed[eighth_at, :] = total.astype(BF16)
        back_lo().start()

    def stage_back_x():
        back_lo(True).wait_recv()
        for k in (1, 2, 3):
            back_x(k).start()

    def stage_back_core():
        for k in (1, 2, 3):
            back_x(k, True).wait_recv()
        back_core().start()

    def widen(i, c):
        r = pl.ds(pl.multiple_of(i * 512, 512), 512)
        grad_o[r, :] = dot(cot_t[r, :], ctx[...])
        return c

    def widen_q(i, c):
        r = pl.ds(pl.multiple_of(i * 512, 512), 512)
        grad_q[r, :] = dot(tok_t[r, :], grad_j[...])
        return c

    def outward(i, c):
        r = pl.ds(pl.multiple_of(i * 512, 512), 512)
        part[:, r] = dot_nt(ctx[...], wo[r, :]).astype(BF16)
        return c

    chunks = tok.shape[1] // 512
    lax.fori_loop(0, chunks, widen, 0)
    rs_far(1)
    ag_end(1)
    lax.fori_loop(0, chunks, outward, 0)
    mx_core().start()
    rs_three(1)
    back[...] = dot(cot[...], wo[...]).astype(BF16)
    retreat(0)
    rs_near(1, 2)
    retreat(1)
    lax.fori_loop(0, chunks, widen_q, 0)
    rs_far(0)
    rs_near(1, 1)
    stage_x()
    rs_three(0)
    rs_out(1)
    stage_lo()
    rs_near(0, 2)
    stage_back()
    rs_near(0, 1)
    stage_back_x()
    rs_out(0)
    stage_back_core()
    rs_end(1, go_out)
    rs_end(0, gq_out)
    back_core(True).wait_recv()
    mixed_out[...] = mixed[...]

    for p in (0, 1):
        ag_drain(p)
        rs_drain(p)
    mx_core().wait_send()
    mx_lo().wait_send()
    back_lo().wait_send()
    back_core().wait_send()
    for k in (1, 2, 3):
        mx_x(k).wait_send()
        back_x(k).wait_send()


def local(tokens, doc_ids, qkv_weight, out_weight, cotangent):
    length, width = tokens.shape
    rows, _, feature = qkv_weight.shape
    joined_width = 3 * feature
    heads = feature // HD
    frequency = 10000.0 ** (-2.0 * np.arange(HD // 2) / HD)
    angles = np.arange(length)[:, None] * frequency[None, :]
    cosine = jnp.asarray(np.concatenate([np.cos(angles), np.cos(angles)], axis=1), F32)
    sine = jnp.asarray(np.concatenate([-np.sin(angles), np.sin(angles)], axis=1), F32)
    vmem = pl.BlockSpec(memory_space=pltpu.VMEM)
    hbm = pl.BlockSpec(memory_space=pl.ANY)
    dma = pltpu.SemaphoreType.DMA
    half = length // NC
    mixed, grad_q, grad_o = pl.pallas_call(
        kernel,
        out_shape=(
            jax.ShapeDtypeStruct((length, width), BF16),
            jax.ShapeDtypeStruct((rows, joined_width), F32),
            jax.ShapeDtypeStruct((rows, feature), F32),
        ),
        in_specs=[hbm, hbm] + [vmem] * 6,
        out_specs=(vmem, vmem, vmem),
        scratch_shapes=[
            pltpu.VMEM((length, width), BF16),
            pltpu.VMEM((length, width), BF16),
            pltpu.VMEM((width, length), BF16),
            pltpu.VMEM((width, length), BF16),
            pltpu.VMEM((width, joined_width), BF16),
            pltpu.VMEM((width, feature), BF16),
            pltpu.VMEM((length, joined_width), BF16),
            pltpu.VMEM((length, feature), BF16),
            pltpu.VMEM((length, feature), BF16),
            pltpu.VMEM((heads, length, length), F32),
            pltpu.VMEM((heads, length, HD), F32),
            pltpu.VMEM((heads, length, HD), F32),
            pltpu.VMEM((length, joined_width), BF16),
            pltpu.VMEM((width, joined_width), F32),
            pltpu.VMEM((width, feature), F32),
            pltpu.VMEM((2, 4, NZ, rows, joined_width), BF16),
            pltpu.VMEM((2, 4, NZ, rows, joined_width), BF16),
            pltpu.VMEM((2, 4, NZ, rows, feature), BF16),
            pltpu.VMEM((2, 4, NZ, rows, feature), BF16),
            pltpu.VMEM((NZ, rows, joined_width), BF16),
            pltpu.VMEM((NZ, rows, joined_width), BF16),
            pltpu.VMEM((NZ, rows, feature), BF16),
            pltpu.VMEM((NZ, rows, feature), BF16),
            pltpu.VMEM((length, width), BF16),
            pltpu.VMEM((half, width), BF16),
            pltpu.VMEM((half, width), BF16),
            pltpu.VMEM((NX - 1, half // NX, width), BF16),
            pltpu.VMEM((half // NX, width), BF16),
            pltpu.VMEM((half // NX // NL, width), BF16),
            pltpu.VMEM((length, width), BF16),
            dma((2,)),
            dma((2, 2, 4, NZ)),
            dma((2, 2, 4, NZ)),
            dma((2, NZ)),
            dma((2, NZ)),
            dma((2, 2, 4, NZ)),
            dma((2, 2, 4, NZ)),
            dma((2, NZ)),
            dma((2, NZ)),
            dma((10,)),
            dma((10,)),
        ],
        compiler_params=pltpu.CompilerParams(
            collective_id=0, has_side_effects=True, vmem_limit_bytes=56 * 1024 * 1024
        ),
        name="layer",
    )(
        tokens,
        cotangent,
        qkv_weight.reshape(rows, joined_width),
        out_weight.T,
        doc_ids.reshape(length, 1),
        doc_ids.reshape(1, length),
        cosine,
        sine,
    )
    return mixed, grad_q.reshape(rows, 3, feature), grad_o.T


def solution(mesh):
    placed = (
        P("blk", None),
        P("blk"),
        P("blk", None, "tensor"),
        P("tensor", "blk"),
        P("blk", None),
    )
    return jax.shard_map(
        local,
        mesh=mesh,
        in_specs=placed,
        out_specs=(P("blk", None), P("blk", None, "tensor"), P("tensor", "blk")),
        check_vma=False,
    )
```

time: 720 us -> 145 us (0.20)
  waiting for transfers between devices: 467 us -> 0 us
  Pallas kernels: 0 us -> 135 us
  starting transfers between devices: 122 us -> 0 us
  other arithmetic: 64.8 us -> 0 us
  matrix products: 19 us -> 0 us
  local copies, waits for them, and re-layouts: 24.5 us -> 7.81 us
  between operations: 13.9 us -> 0.64 us
    ppermute x62 -> x0, waiting for transfers between devices: 278 us -> none  [passed_along(): lax.ppermute(x, axis, [(i, (i + by) % length) for i in range(length)])]
    all_gather x2 -> x0, waiting for transfers between devices: 188 us -> none  [the longest x1 97.7 us: local(): weight_piece = lax.all_gather(qkv_weight, 'blk', axis=0, tiled=True)]
    pallas_call x0 -> x1, Pallas kernels: none -> 135 us  [local(): pl.pallas_call(kernel, out_shape=(jax.ShapeDtypeStruct((length, width), B...]
    ppermute x62 -> x0, starting transfers between devices: 122 us -> none  [passed_along(): lax.ppermute(x, axis, [(i, (i + by) % length) for i in range(length)])]
    add x62 -> x0, other arithmetic: 57.9 us -> none  [add_pair(): return (left_pair[0] + right_pair[0], left_pair[1] + right_pair[1])]
    dot_general x11 -> x0, matrix products: 19 us -> none  [the longest x1 4.34 us: local(): lax.dot_general(tokens, grad_joined, (((0,), (0,)), ((), ())), preferred_...]
    dot_general x2 -> x0, local copies, waits for them, and re-layouts: 12.4 us -> none  [the longest x1 9.07 us: local(): lax.dot_general(tokens, grad_joined, (((0,), (0,)), ((), ())), preferred_...]
  transfers between devices with their start and end apart: 65 -> 0, of which waited for: 64 -> 0; matrix products, arithmetic and copies ran while one was open for 12% -> 0% of each run, Pallas kernels for 0% -> 0%
where the time goes in v1:
time: 145 us; the launch traced here: 143 us
  Pallas kernels  135 us (93%)
  local copies, waits for them, and re-layouts  7.81 us (5%)
    pallas_call x1, Pallas kernels, local(): pl.pallas_call(kernel, out_shape=(jax.ShapeDtypeStruct((length, width), B...  135 us
    unnamed x4, local copies, waits for them, and re-layouts  3.13 us

profile of v1, /device:TPU:6, one launch (start us, length us, event | category | flops | bytes accessed | tf_op | source)
XLA Modules:
  0.0 143.3 jit_solution(4659752109222001274)
XLA Ops:
  0.6 1.6 %copy.16 = bf16[3,10,8,256]{3,2,0,1:T(8,128)(2,1)} copy(bf16[3,10,8,256]{3,2,1,0:T(8,128)(2,1)} %bitcast.13) | data formatting | bytes 245760 | tf_op jit(solution)/shard_map/reshape | solution.py:511
  2.2 1.5 %copy.13.doc_col = s32[256,1]{1,0:T(8,128)} copy(s32[256,1]{0,1:T(1,128)} %bitcast.16) | data formatting | bytes 2048 | tf_op jit(solution)/shard_map/reshape | solution.py:513
  3.7 134.8 %layer.1 = (bf16[256,2560]{1,0:T(8,128)(2,1)}, f32[80,768]{1,0:T(8,128)}, f32[80,256]{1,0:T(8,128)}) custom-call(bf16[256,2560]{1,0:T(8,128)(2,1)} %tokens_hbm.1, bf16[256,2560]{1,0:T(8,128)(2,1)} %cot_hbm.1, bf16[80,768]{1,0:T(8,128)(2,1)} %bitcast.10, bf16[80,256]{1,0:T(8,128)(2,1)} %bitcast.15, s32[256,1]{1,0:T(8,128)} %copy.13.doc_col, ...), custom_call_target="tpu_custom_call" | custom-call | tf_op jit(solution)/shard_map/layer/pallas_call | solution.py:452
  138.5 1.7 %copy.18 = f32[10,3,8,256]{3,2,0,1:T(8,128)} copy(f32[10,3,8,256]{3,2,1,0:T(8,128)} %bitcast.12) | data formatting | bytes 491520 | tf_op jit(solution)/shard_map/reshape | solution.py:518
  140.2 0.0 copy-start
  140.2 2.5 %copy.21 = bf16[256,2560]{1,0:T(8,128)(2,1)} copy(bf16[256,2560]{1,0:T(8,128)(2,1)} %get-tuple-element.18) | data formatting | bytes 2621440
  142.6 0.0 copy-done
  142.6 0.6 copy.22
Async XLA Ops:
  140.2 2.5 %copy-start = (f32[80,256]{1,0:T(8,128)S(1)}, f32[80,256]{1,0:T(8,128)}, u32[]{:S(2)}) copy-start(f32[80,256]{1,0:T(8,128)} %get-tuple-element.8) | copy-start | bytes 245764

commit v2 on v1

--- a/solution.py
+++ b/solution.py
@@ -32,19 +32,20 @@
 
 
 def kernel(
-    tokens_hbm, cot_hbm, wq_in, wo_in, doc_col, doc_row, cos_in, sin_in,
+    tokens_hbm, cot_hbm, wq_in, wo_in, doc_row, cos_in, sin_in,
     mixed_out, gq_out, go_out,
     tok, cot, tok_t, cot_t, wq, wo, joined, ctx, back, probs, q_rot, k_rot, grad_j,
-    grad_q, grad_o, sq, rq, so, ro, zsq, zrq, zso, zro,
+    grad_q, grad_o, sq, rq, so, ro, zsq, zrq, zso, zro, doc_col,
     part, part_c, sum_c, recv_x, sum_x, recv_l, mixed,
-    load_sem, ag_ss, ag_rs, agz_ss, agz_rs, rs_ss, rs_rs, rsz_ss, rsz_rs, mx_ss, mx_rs,
+    load_sem, ag_ss, ag_rs, agz_ss, agz_rs, rs_ss, rs_rs, rsz_ss, rsz_rs,
+    go_ss, go_rs, goz_ss, goz_rs, gr_ss, gr_rs, grz_ss, grz_rs, mx_ss, mx_rs,
 ):
     blk = lax.axis_index("blk")
     ten = lax.axis_index("tensor")
     zh, y = blk // NY, blk % NY
     x, rest = ten // (NL * NC), ten % (NL * NC)
     lo, core = rest // NC, rest % NC
-    rows = wq_in.shape[0]
+    rows, third = wq_in.shape[1], wq_in.shape[2]
     length = tok.shape[0]
 
     def at_z(k):
@@ -74,7 +75,8 @@
         return pl.ds(pl.multiple_of((z * NY + yy) * rows, 16), rows)
 
     mine = row_at(zh, y)
-    wq[mine, :] = wq_in[...]
+    for c in range(3):
+        wq[mine, c * third:(c + 1) * third] = wq_in[c]
     wo[mine, :] = wo_in[...]
     pl.semaphore_wait(barrier, len(peers))
 
@@ -84,83 +86,99 @@
             device_id=peer, device_id_type=pl.DeviceIdType.MESH,
         )
 
-    gathered = (wq, wo)
-
-    def ag_z(p, k):
-        w = gathered[p]
-        return remote(w.at[mine, :], w.at[mine, :], agz_ss.at[p, k], agz_rs.at[p, k], at_z(k))
-
-    def ag_z_got(p, k):
-        w = gathered[p]
-        here = row_at((zh - k + NZ) % NZ, y)
-        return remote(w.at[here, :], w.at[here, :], agz_ss.at[p, k], agz_rs.at[p, k], at_z(k))
-
-    def ag_y(p, way, s, j, got):
-        w = gathered[p]
+    def long(way, j):
+        return j % 2 == way
+
+    def ag_z(k):
+        return remote(wq.at[mine, :], wq.at[mine, :], agz_ss.at[k], agz_rs.at[k], at_z(k))
+
+    def ag_y(way, s, j, got):
         sign = 1 if way == 0 else -1
         off = s + 1 if got else s
         here = row_at((zh - j + NZ) % NZ, (y - sign * off + 2 * NY) % NY)
         return remote(
-            w.at[here, :], w.at[here, :], ag_ss.at[p, way, s, j], ag_rs.at[p, way, s, j],
+            wq.at[here, :], wq.at[here, :], ag_ss.at[way, s, j], ag_rs.at[way, s, j],
             up if way == 0 else down,
         )
 
-    def long_js(way):
-        return (0, 2) if way == 0 else (1, 3)
-
-    def ag_first(p):
-        for k in (1, 2, 3):
-            ag_z(p, k).start()
-
-        for way in (0, 1):
-            ag_y(p, way, 0, 0, False).start()
-
-        def body(j, c):
-            ag_z_got(p, j).wait_recv()
-            for way in (0, 1):
-                ag_y(p, way, 0, j, False).start()
-            return c
-
-        lax.fori_loop(1, NZ, body, 0)
-
-    def ag_mid(p, s):
-        def body(j, c):
-            for way in (0, 1):
-                ag_y(p, way, s - 1, j, True).wait_recv()
-                ag_y(p, way, s, j, False).start()
-            return c
-
-        lax.fori_loop(0, NZ, body, 0)
-
-    def ag_last(p):
+    def ag_step(j, s):
+        if s == 0 and j > 0:
+            here = row_at((zh - j + NZ) % NZ, y)
+            remote(wq.at[here, :], wq.at[here, :], agz_ss.at[j], agz_rs.at[j], at_z(j)).wait_recv()
+        for way in (0, 1):
+            if s > 0:
+                ag_y(way, s - 1, j, True).wait_recv()
+            if s < 3 or long(way, j):
+                ag_y(way, s, j, False).start()
+
+    def ag_end():
         for j in range(NZ):
             for way in (0, 1):
-                ag_y(p, way, 2, j, True).wait_recv()
-                if j in long_js(way):
-                    ag_y(p, way, 3, j, False).start()
-
-    def ag_end(p):
+                if long(way, j):
+                    ag_y(way, 3, j, True).wait_recv()
+
+    def ag_drain():
+        for k in (1, 2, 3):
+            ag_z(k).wait_send()
         for j in range(NZ):
             for way in (0, 1):
-                if j in long_js(way):
-                    ag_y(p, way, 3, j, True).wait_recv()
-
-    def ag_drain(p):
-        for k in (1, 2, 3):
-            ag_z(p, k).wait_send()
-
-        def body(j, c):
-            for way in (0, 1):
-                for s in range(3):
-                    ag_y(p, way, s, j, False).wait_send()
+                for s in range(4):
+                    if s < 3 or long(way, j):
+                        ag_y(way, s, j, False).wait_send()
+
+    def go_y(way, s, got):
+        sign = 1 if way == 0 else -1
+        off = s + 1 if got else s
+        here = row_at(zh, (y - sign * off + NY) % NY)
+        return remote(
+            wo.at[here, :], wo.at[here, :], go_ss.at[way, s], go_rs.at[way, s],
+            up if way == 0 else down,
+        )
+
+    def go_z(r, k, got=False):
+        yy = (y - r + NY) % NY
+        here = row_at((zh - k + NZ) % NZ if got else zh, yy)
+        return remote(
+            wo.at[here, :], wo.at[here, :], goz_ss.at[r, k], goz_rs.at[r, k], at_z(k)
+        )
+
+    def go_step(s):
+        for way in (0, 1):
+            if s > 0 and (s < 4 or way == 0):
+                go_y(way, s - 1, True).wait_recv()
+            if s < (4, 3)[way]:
+                go_y(way, s, False).start()
+
+    def go_spread(s):
+        for r in (s,) if s in (0, 4) else (s, NY - s):
+            for k in (1, 3, 2):
+                go_z(r, k).start()
+
+    def go_end():
+        def body(r, c):
+            for k in (1, 2, 3):
+                go_z(r, k, True).wait_recv()
             return c
 
-        lax.fori_loop(0, NZ, body, 0)
-        for way in (0, 1):
-            for j in long_js(way):
-                ag_y(p, way, 3, j, False).wait_send()
-
-    ag_first(0)
+        lax.fori_loop(0, NY, body, 0)
+
+    def go_drain():
+        for way in (0, 1):
+            for s in range((4, 3)[way]):
+                go_y(way, s, False).wait_send()
+
+        def body(r, c):
+            for k in (1, 2, 3):
+                go_z(r, k).wait_send()
+            return c
+
+        lax.fori_loop(0, NY, body, 0)
+
+    ag_z(1).start()
+    ag_z(3).start()
+    ag_step(0, 0)
+    ag_z(2).start()
+    go_step(0)
     load_tok.wait()
     load_cot.wait()
 
@@ -170,12 +188,33 @@
         cot_t[cols, :] = cot[:, cols].T
         return c
 
-    ag_mid(0, 1)
+    ag_step(0, 1)
+    go_step(1)
+    ag_step(1, 0)
     lax.fori_loop(0, tok.shape[1] // 256, flip, 0)
-    ag_mid(0, 2)
-    ag_last(0)
-    ag_first(1)
-    ag_end(0)
+    doc_col[...] = jnp.broadcast_to(doc_row[...], (length, length)).T
+    ag_step(0, 2)
+    ag_step(3, 0)
+    ag_step(1, 1)
+    go_step(2)
+    ag_step(2, 0)
+    go_spread(0)
+    go_spread(1)
+    ag_step(0, 3)
+    ag_step(3, 1)
+    go_step(3)
+    go_spread(2)
+    ag_step(1, 2)
+    ag_step(2, 1)
+    go_step(4)
+    go_spread(3)
+    go_spread(4)
+    ag_step(3, 2)
+    ag_step(1, 3)
+    ag_step(2, 2)
+    ag_step(3, 3)
+    ag_step(2, 3)
+    ag_end()
 
     cosine, sine = cos_in[...], sin_in[...]
     scale = 1.0 / math.sqrt(HD)
@@ -215,95 +254,107 @@
         grad_j[:, width + h * HD:width + (h + 1) * HD] = turned(d_k, cosine, -sine).astype(BF16)
         grad_j[:, 2 * width + h * HD:2 * width + (h + 1) * HD] = d_val.astype(BF16)
 
-    project()
-    ag_mid(1, 1)
-    attend(0)
-    ag_mid(1, 2)
-    attend(1)
-    ag_last(1)
-
-    grads, sends, recvs = (grad_q, grad_o), (sq, so), (rq, ro)
-    z_sends, z_recvs = (zsq, zso), (zrq, zro)
-
-    def rs_y(p, way, d, j):
+    def rs_y(way, d, j):
         return remote(
-            sends[p].at[way, d - 1, j], recvs[p].at[way, d - 1, j],
-            rs_ss.at[p, way, d - 1, j], rs_rs.at[p, way, d - 1, j],
+            sq.at[way, d - 1, j], rq.at[way, d - 1, j], rs_ss.at[way, d - 1, j], rs_rs.at[way, d - 1, j],
             up if way == 0 else down,
         )
 
-    def rs_own(p, way, d, j):
-        sign = 1 if way == 0 else -1
-        return grads[p][row_at((zh - j + NZ) % NZ, (y + sign * d + NY) % NY), :]
-
-    def rs_far(p):
-        for way in (0, 1):
-            for j in long_js(way):
-                sends[p][way, 3, j] = rs_own(p, way, 4, j).astype(BF16)
-                rs_y(p, way, 4, j).start()
-
-    def rs_three(p):
-        for j in (1, 2, 3, 0):
+    def rs_step(j, u):
+        d = 4 - u
+        for way in (0, 1):
+            if d == 4 and not long(way, j):
+                continue
+            sign = 1 if way == 0 else -1
+            own = grad_q[row_at((zh - j + NZ) % NZ, (y + sign * d + NY) % NY), :]
+            if d < 3 or (d == 3 and long(way, j)):
+                rs_y(way, d + 1, j).wait_recv()
+                own = own + rq[way, d, j].astype(F32)
+            sq[way, d - 1, j] = own.astype(BF16)
+            rs_y(way, d, j).start()
+
+    def rs_here(j):
+        for way in (0, 1):
+            rs_y(way, 1, j).wait_recv()
+        own = grad_q[row_at((zh - j + NZ) % NZ, y), :]
+        return own + rq[0, 0, j].astype(F32) + rq[1, 0, j].astype(F32)
+
+    def rs_z(j):
+        return remote(zsq.at[j], zrq.at[j], rsz_ss.at[j], rsz_rs.at[j], at_z(NZ - j))
+
+    def rs_out(j):
+        zsq[j] = rs_here(j).astype(BF16)
+        rs_z(j).start()
+
+    def rs_end():
+        total = rs_here(0)
+        for j in (1, 2, 3):
+            rs_z(j).wait_recv()
+            total = total + zrq[j].astype(F32)
+        for c in range(3):
+            gq_out[c] = total[:, c * third:(c + 1) * third]
+
+    def rs_drain():
+        for j in range(NZ):
+            if j > 0:
+                rs_z(j).wait_send()
             for way in (0, 1):
-                own = rs_own(p, way, 3, j)
-                if j in long_js(way):
-                    rs_y(p, way, 4, j).wait_recv()
-                    own = own + recvs[p][way, 3, j].astype(F32)
-                sends[p][way, 2, j] = own.astype(BF16)
-                rs_y(p, way, 3, j).start()
-
-    def rs_near(p, d):
-        def body(i, c):
-            j = (i + 1) % NZ
-            for way in (0, 1):
-                rs_y(p, way, d + 1, j).wait_recv()
-                own = rs_own(p, way, d, j) + recvs[p][way, d, j].astype(F32)
-                sends[p][way, d - 1, j] = own.astype(BF16)
-                rs_y(p, way, d, j).start()
+                for d in (1, 2, 3, 4):
+                    if d < 4 or long(way, j):
+                        rs_y(way, d, j).wait_send()
+
+    def gr_z(r, k):
+        return remote(zso.at[r, k], zro.at[r, k], grz_ss.at[r, k], grz_rs.at[r, k], at_z(k))
+
+    def gr_spread(r):
+        for k in (1, 3, 2):
+            zso[r, k] = grad_o[row_at((zh + k) % NZ, (y + r) % NY), :].astype(BF16)
+            gr_z(r, k).start()
+
+    def gr_own(r):
+        total = grad_o[row_at(zh, (y + r) % NY), :]
+        for k in (1, 2, 3):
+            gr_z(r, k).wait_recv()
+            total = total + zro[r, k].astype(F32)
+        return total
+
+    def gr_y(way, d):
+        return remote(
+            so.at[way, d - 1], ro.at[way, d - 1], gr_ss.at[way, d - 1], gr_rs.at[way, d - 1],
+            up if way == 0 else down,
+        )
+
+    def gr_step(u):
+        d = 4 - u
+        for way in (0, 1):
+            if d == 4 and way == 1:
+                continue
+            own = gr_own(d if way == 0 else NY - d)
+            if d < 3 or (d == 3 and way == 0):
+                gr_y(way, d + 1).wait_recv()
+                own = own + ro[way, d].astype(F32)
+            so[way, d - 1] = own.astype(BF16)
+            gr_y(way, d).start()
+
+    def gr_end():
+        total = gr_own(0)
+        for way in (0, 1):
+            gr_y(way, 1).wait_recv()
+            total = total + ro[way, 0].astype(F32)
+        go_out[...] = total
+
+    def gr_drain():
+        for way in (0, 1):
+            for d in (1, 2, 3, 4):
+                if d < 4 or way == 0:
+                    gr_y(way, d).wait_send()
+
+        def body(r, c):
+            for k in (1, 2, 3):
+                gr_z(r, k).wait_send()
             return c
 
-        lax.fori_loop(0, NZ, body, 0)
-
-    def rs_z(p, j):
-        return remote(
-            z_sends[p].at[j], z_recvs[p].at[j], rsz_ss.at[p, j], rsz_rs.at[p, j], at_z(NZ - j)
-        )
-
-    def rs_here(p, j):
-        for way in (0, 1):
-            rs_y(p, way, 1, j).wait_recv()
-        own = grads[p][row_at((zh - j + NZ) % NZ, y), :]
-        return own + recvs[p][0, 0, j].astype(F32) + recvs[p][1, 0, j].astype(F32)
-
-    def rs_out(p):
-        def body(j, c):
-            z_sends[p][j] = rs_here(p, j).astype(BF16)
-            rs_z(p, j).start()
-            return c
-
-        lax.fori_loop(1, NZ, body, 0)
-
-    def rs_end(p, out):
-        total = rs_here(p, 0)
-        for j in (1, 2, 3):
-            rs_z(p, j).wait_recv()
-            total = total + z_recvs[p][j].astype(F32)
-        out[...] = total
-
-    def rs_drain(p):
-        for j in (1, 2, 3):
-            rs_z(p, j).wait_send()
-
-        def body(j, c):
-            for way in (0, 1):
-                for d in (1, 2, 3):
-                    rs_y(p, way, d, j).wait_send()
-            return c
-
-        lax.fori_loop(0, NZ, body, 0)
-        for way in (0, 1):
-            for j in long_js(way):
-                rs_y(p, way, 4, j).wait_send()
+        lax.fori_loop(0, NY, body, 0)
 
     half = length // NC
     quarter = half // NX
@@ -395,38 +446,66 @@
         part[:, r] = dot_nt(ctx[...], wo[r, :]).astype(BF16)
         return c
 
+    def leave(got):
+        at = half_at
+        if got:
+            at = pl.ds(pl.multiple_of((1 - core) * half, 16), half)
+        return pltpu.make_async_copy(mixed.at[at, :], mixed_out.at[at, :], load_sem.at[got])
+
     chunks = tok.shape[1] // 512
+    project()
+    attend(0)
+    attend(1)
     lax.fori_loop(0, chunks, widen, 0)
-    rs_far(1)
-    ag_end(1)
+    for r in (4, 3, 5, 2, 6, 1, 7, 0):
+        gr_spread(r)
+    go_end()
     lax.fori_loop(0, chunks, outward, 0)
     mx_core().start()
-    rs_three(1)
     back[...] = dot(cot[...], wo[...]).astype(BF16)
     retreat(0)
-    rs_near(1, 2)
     retreat(1)
     lax.fori_loop(0, chunks, widen_q, 0)
-    rs_far(0)
-    rs_near(1, 1)
+    rs_step(2, 0)
+    rs_step(1, 0)
     stage_x()
-    rs_three(0)
+    rs_step(2, 1)
+    rs_step(3, 0)
+    gr_step(0)
+    rs_step(1, 1)
+    rs_step(2, 2)
+    rs_step(0, 0)
+    gr_step(1)
+    stage_lo()
+    rs_step(3, 1)
+    rs_step(1, 2)
+    rs_step(2, 3)
+    stage_back()
+    rs_step(0, 1)
+    gr_step(2)
+    rs_step(3, 2)
+    rs_out(2)
+    rs_step(1, 3)
+    stage_back_x()
+    rs_step(0, 2)
+    rs_step(3, 3)
     rs_out(1)
-    stage_lo()
-    rs_near(0, 2)
-    stage_back()
-    rs_near(0, 1)
-    stage_back_x()
-    rs_out(0)
+    gr_step(3)
+    rs_step(0, 3)
+    rs_out(3)
     stage_back_core()
-    rs_end(1, go_out)
-    rs_end(0, gq_out)
+    leave(0).start()
+    gr_end()
     back_core(True).wait_recv()
-    mixed_out[...] = mixed[...]
-
-    for p in (0, 1):
-        ag_drain(p)
-        rs_drain(p)
+    leave(1).start()
+    rs_end()
+
+    leave(0).wait()
+    leave(1).wait()
+    ag_drain()
+    go_drain()
+    rs_drain()
+    gr_drain()
     mx_core().wait_send()
     mx_lo().wait_send()
     back_lo().wait_send()
@@ -453,11 +532,11 @@
         kernel,
         out_shape=(
             jax.ShapeDtypeStruct((length, width), BF16),
-            jax.ShapeDtypeStruct((rows, joined_width), F32),
+            jax.ShapeDtypeStruct((3, rows, feature), F32),
             jax.ShapeDtypeStruct((rows, feature), F32),
         ),
-        in_specs=[hbm, hbm] + [vmem] * 6,
-        out_specs=(vmem, vmem, vmem),
+        in_specs=[hbm, hbm] + [vmem] * 5,
+        out_specs=(hbm, vmem, vmem),
         scratch_shapes=[
             pltpu.VMEM((length, width), BF16),
             pltpu.VMEM((length, width), BF16),
@@ -476,12 +555,13 @@
             pltpu.VMEM((width, feature), F32),
             pltpu.VMEM((2, 4, NZ, rows, joined_width), BF16),
             pltpu.VMEM((2, 4, NZ, rows, joined_width), BF16),
-            pltpu.VMEM((2, 4, NZ, rows, feature), BF16),
-            pltpu.VMEM((2, 4, NZ, rows, feature), BF16),
+            pltpu.VMEM((2, 4, rows, feature), BF16),
+            pltpu.VMEM((2, 4, rows, feature), BF16),
             pltpu.VMEM((NZ, rows, joined_width), BF16),
             pltpu.VMEM((NZ, rows, joined_width), BF16),
-            pltpu.VMEM((NZ, rows, feature), BF16),
-            pltpu.VMEM((NZ, rows, feature), BF16),
+            pltpu.VMEM((NY, NZ, rows, feature), BF16),
+            pltpu.VMEM((NY, NZ, rows, feature), BF16),
+            pltpu.VMEM((length, length), jnp.int32),
             pltpu.VMEM((length, width), BF16),
             pltpu.VMEM((half, width), BF16),
             pltpu.VMEM((half, width), BF16),
@@ -490,14 +570,22 @@
             pltpu.VMEM((half // NX // NL, width), BF16),
             pltpu.VMEM((length, width), BF16),
             dma((2,)),
-            dma((2, 2, 4, NZ)),
-            dma((2, 2, 4, NZ)),
-            dma((2, NZ)),
-            dma((2, NZ)),
-            dma((2, 2, 4, NZ)),
-            dma((2, 2, 4, NZ)),
-            dma((2, NZ)),
-            dma((2, NZ)),
+            dma((2, 4, NZ)),
+            dma((2, 4, NZ)),
+            dma((NZ,)),
+            dma((NZ,)),
+            dma((2, 4, NZ)),
+            dma((2, 4, NZ)),
+            dma((NZ,)),
+            dma((NZ,)),
+            dma((2, 4)),
+            dma((2, 4)),
+            dma((NY, NZ)),
+            dma((NY, NZ)),
+            dma((2, 4)),
+            dma((2, 4)),
+            dma((NY, NZ)),
+            dma((NY, NZ)),
             dma((10,)),
             dma((10,)),
         ],
@@ -508,14 +596,13 @@
     )(
         tokens,
         cotangent,
-        qkv_weight.reshape(rows, joined_width),
+        qkv_weight.transpose(1, 0, 2),
         out_weight.T,
-        doc_ids.reshape(length, 1),
         doc_ids.reshape(1, length),
         cosine,
         sine,
     )
-    return mixed, grad_q.reshape(rows, 3, feature), grad_o.T
+    return mixed, grad_q.transpose(1, 0, 2), grad_o.T
 
 
 def solution(mesh):

time: 145 us -> 125 us (0.86)
  the two profiles are of different devices: /device:TPU:6 before, /device:TPU:64 now
where the time goes in v2:
time: 125 us
  Pallas kernels  121 us (97%)
  local copies, waits for them, and re-layouts  3.84 us (3%)
    pallas_call x1, Pallas kernels, local(): pl.pallas_call(kernel, out_shape=(jax.ShapeDtypeStruct((length, width), B...  121 us
    unnamed x7, local copies, waits for them, and re-layouts  3.84 us

profile of v2, /device:TPU:64, one launch (start us, length us, event | category | flops | bytes accessed | tf_op | source)
XLA Modules:
  0.0 125.1 jit_solution(5297774414163672291)
XLA Ops:
  0.6 120.6 %layer.1 = (bf16[256,2560]{1,0:T(8,128)(2,1)}, f32[3,80,256]{2,1,0:T(8,128)}, f32[80,256]{1,0:T(8,128)}) custom-call(bf16[256,2560]{1,0:T(8,128)(2,1)} %tokens_hbm.1, bf16[256,2560]{1,0:T(8,128)(2,1)} %cot_hbm.1, bf16[3,80,256]{2,1,0:T(8,128)(2,1)} %bitcast.6, bf16[80,256]{1,0:T(8,128)(2,1)} %bitcast.8, s32[1,256]{1,0:T(1,128)} %bitcast.9, ...), custom_call_target="tpu_custom_call" | custom-call | tf_op jit(solution)/shard_map/layer/pallas_call | solution.py:531
  121.2 0.0 copy-start
  121.2 0.0 copy-start.1
  121.3 2.5 %copy.13 = bf16[256,2560]{1,0:T(8,128)(2,1)} copy(bf16[256,2560]{1,0:T(8,128)(2,1)} %get-tuple-element.12) | data formatting | bytes 2621440
  123.8 0.0 copy-done
  123.8 0.7 copy.14
  124.5 0.0 copy-done.1
  124.5 0.6 copy.15
Async XLA Ops:
  121.2 2.5 %copy-start = (f32[3,80,256]{2,1,0:T(8,128)S(1)}, f32[3,80,256]{2,1,0:T(8,128)}, u32[]{:S(2)}) copy-start(f32[3,80,256]{2,1,0:T(8,128)} %get-tuple-element.7) | copy-start | bytes 737284
  121.2 3.2 %copy-start.1 = (f32[80,256]{1,0:T(8,128)S(1)}, f32[80,256]{1,0:T(8,128)}, u32[]{:S(2)}) copy-start(f32[80,256]{1,0:T(8,128)} %get-tuple-element.8) | copy-start | bytes 245764

commit v3 on v0

v3 whole, which is shorter than its diff:
```python
import math

import jax
import jax.numpy as jnp
import numpy as np
from jax import lax
from jax.experimental import pallas as pl
from jax.experimental.pallas import tpu as pltpu
from jax.sharding import PartitionSpec as P

HD = 128
NZ, NY = 4, 8
NX, NL, NC = 4, 2, 2
F32 = jnp.float32
BF16 = jnp.bfloat16
HIGHEST = lax.Precision.HIGHEST
NT = (((1,), (1,)), ((), ()))


def dot(a, b):
    return jnp.dot(a, b, preferred_element_type=F32)


def dot_nt(a, b):
    return lax.dot_general(a, b, NT, preferred_element_type=F32)


def turned(x, cosine, sine):
    half = x.shape[1] // 2
    swapped = jnp.concatenate([x[:, half:], x[:, :half]], axis=1)
    return x * cosine + swapped * sine


def kernel(
    tokens_hbm, cot_hbm, wq_in, wo_in, doc_in, cos_in, sin_in,
    mixed_out, gq_out, go_out,
    tok, cot, tok_t, cot_t, docs, staged, w, joined, ctx, back, probs, q_rot, k_rot, grad_j,
    grad, sq, rq, zs, zr, part, part_c, sum_c, recv_x, sum_x, recv_z, mixed,
    load_sem, ag_ss, ag_rs, agz_ss, agz_rs, rs_ss, rs_rs, rsz_ss, rsz_rs, tk_ss, tk_rs, mx_ss, mx_rs,
):
    blk = lax.axis_index("blk")
    ten = lax.axis_index("tensor")
    zh, y = blk // NY, blk % NY
    x, rest = ten // (NL * NC), ten % (NL * NC)
    lo, core = rest // NC, rest % NC
    rows = wq_in.shape[1]
    length = tok.shape[1]
    width = tok.shape[2]
    pick = zh % 2

    def at_z(k):
        return (((zh + k) % NZ) * NY + y, ten)

    def at_y(step):
        return (zh * NY + (y + step + NY) % NY, ten)

    def at_x(k):
        return (blk, ((x + k) % NX) * (NL * NC) + rest)

    up, down = at_y(1), at_y(-1)
    core_peer = (blk, ten + 1 - 2 * core)
    other_lo = ten + NC - 2 * NC * lo
    lo_peer = (blk, other_lo)
    other_blk = blk + NY - 2 * NY * pick
    partner = (other_blk, ten)
    partner_lo = (other_blk, other_lo)

    load_tok = pltpu.make_async_copy(tokens_hbm, tok.at[0], load_sem.at[0])
    load_cot = pltpu.make_async_copy(cot_hbm, cot.at[0], load_sem.at[1])
    load_tok.start()
    load_cot.start()

    barrier = pltpu.get_barrier_semaphore()
    peers = [at_z(k) for k in (1, 2, 3)] + [at_x(k) for k in (1, 2, 3)]
    peers += [up, down, core_peer, lo_peer, partner_lo]
    for peer in peers:
        pl.semaphore_signal(barrier, inc=1, device_id=peer, device_id_type=pl.DeviceIdType.MESH)

    def row_at(z, yy):
        return pl.ds(pl.multiple_of((z * NY + yy) * rows, 16), rows)

    for h in range(2):
        for c in range(3):
            staged[h, :, c * HD:(c + 1) * HD] = wq_in[c, :, h * HD:(h + 1) * HD]
        staged[h, :, 3 * HD:] = wo_in[:, h * HD:(h + 1) * HD]
    mine = row_at(zh, y)
    w[mine, :] = staged[pick]
    docs[0] = jnp.broadcast_to(doc_in[...], docs.shape[1:])
    load_tok.wait()
    load_cot.wait()
    pl.semaphore_wait(barrier, len(peers))

    def remote(src, dst, ss, rs, peer):
        return pltpu.make_async_remote_copy(
            src_ref=src, dst_ref=dst, send_sem=ss, recv_sem=rs,
            device_id=peer, device_id_type=pl.DeviceIdType.MESH,
        )

    def long(way, j):
        return j % 2 == way

    half = length // NC
    quarter = half // NX
    eighth = quarter // NL

    def place(c, xx=None, ll=None):
        if xx is None:
            return pl.ds(pl.multiple_of(c * half, 16), half)
        if ll is None:
            return pl.ds(pl.multiple_of(c * half + xx * quarter, 16), quarter)
        return pl.ds(pl.multiple_of(c * half + xx * quarter + ll * eighth, 16), eighth)

    def tk_copy(i, stage, got=False):
        a = (tok, cot)[i]
        if stage == 0:
            at = place(core, x, lo)
            return remote(a.at[0, at, :], a.at[1, at, :], tk_ss.at[i, 0], tk_rs.at[i, 0], partner)
        if stage == 1:
            at, peer = place(core, x, 1 - lo if got else lo), lo_peer
        elif stage == 5:
            at, peer = place(1 - core if got else core), core_peer
        else:
            k = stage - 1
            at, peer = place(core, (x - k + NX) % NX if got else x), at_x(k)
        return remote(a.at[1, at, :], a.at[1, at, :], tk_ss.at[i, stage], tk_rs.at[i, stage], peer)

    def tk_lo(i):
        tk_copy(i, 0).wait_recv()
        tk_copy(i, 1).start()

    def tk_x(i):
        tk_copy(i, 1, True).wait_recv()
        for stage in (2, 4, 3):
            tk_copy(i, stage).start()

    def tk_core(i):
        for stage in (2, 4, 3):
            tk_copy(i, stage, True).wait_recv()
        tk_copy(i, 5).start()

    def tk_end(i):
        tk_copy(i, 5, True).wait_recv()

    def tk_drain():
        for i in (0, 1):
            for stage in range(6):
                tk_copy(i, stage).wait_send()

    def doc_copy():
        return remote(docs.at[0], docs.at[1], tk_ss.at[0, 6], tk_rs.at[0, 6], partner)

    def ag_z(k):
        return remote(
            staged.at[(zh + k) % 2], w.at[mine, :], agz_ss.at[k], agz_rs.at[k], at_z(k)
        )

    def ag_y(way, s, j, got):
        sign = 1 if way == 0 else -1
        off = s + 1 if got else s
        here = row_at((zh - j + NZ) % NZ, (y - sign * off + 2 * NY) % NY)
        return remote(
            w.at[here, :], w.at[here, :], ag_ss.at[way, s, j], ag_rs.at[way, s, j],
            up if way == 0 else down,
        )

    def ag_step(j, s):
        if s == 0 and j > 0:
            here = row_at((zh - j + NZ) % NZ, y)
            remote(w.at[here, :], w.at[here, :], agz_ss.at[j], agz_rs.at[j], at_z(j)).wait_recv()
        for way in (0, 1):
            if s > 0:
                ag_y(way, s - 1, j, True).wait_recv()
            if s < 3 or long(way, j):
                ag_y(way, s, j, False).start()

    def ag_end():
        for j in range(NZ):
            for way in (0, 1):
                if long(way, j):
                    ag_y(way, 3, j, True).wait_recv()

    def ag_drain():
        for k in (1, 2, 3):
            ag_z(k).wait_send()
        for j in range(NZ):
            for way in (0, 1):
                for s in range(4):
                    if s < 3 or long(way, j):
                        ag_y(way, s, j, False).wait_send()

    def flip(a, a_t, m):
        def body(i, c):
            cols = pl.ds(pl.multiple_of(i * 256, 256), 256)
            a_t[cols, m * length:(m + 1) * length] = a[m, :, cols].T
            return c

        lax.fori_loop(0, width // 256, body, 0)

    cosine, sine = cos_in[...], sin_in[...]
    scale = 1.0 / math.sqrt(HD)

    def rows_of(m):
        return slice(m * length, (m + 1) * length)

    def project(m):
        joined[rows_of(m), :] = dot(tok[m], w[:, :3 * HD]).astype(BF16)

    def attend(m):
        qr = turned(joined[rows_of(m), :HD].astype(F32), cosine, sine)
        kr = turned(joined[rows_of(m), HD:2 * HD].astype(F32), cosine, sine)
        q_rot[m] = qr
        k_rot[m] = kr
        scores = lax.dot_general(qr, kr, NT, precision=HIGHEST, preferred_element_type=F32) * scale
        row = lax.broadcasted_iota(jnp.int32, (length, length), 0)
        col = lax.broadcasted_iota(jnp.int32, (length, length), 1)
        ids = jnp.broadcast_to(docs[m, :1, :], (length, length))
        allowed = (col <= row) & (ids == ids.T)
        scores = jnp.where(allowed, scores, -1e30)
        expo = jnp.exp(scores - jnp.max(scores, axis=1, keepdims=True))
        p = expo / jnp.sum(expo, axis=1, keepdims=True)
        probs[m] = p
        ctx[rows_of(m), :] = dot(p.astype(BF16), joined[rows_of(m), 2 * HD:]).astype(BF16)

    def retreat(m):
        p = probs[m]
        d_out = back[rows_of(m), :]
        d_val = jnp.dot(p.T, d_out.astype(F32), precision=HIGHEST, preferred_element_type=F32)
        d_p = dot_nt(d_out, joined[rows_of(m), 2 * HD:])
        d_s = p * (d_p - jnp.sum(p * d_p, axis=1, keepdims=True)) * scale
        d_q = jnp.dot(d_s, k_rot[m], precision=HIGHEST, preferred_element_type=F32)
        d_k = jnp.dot(d_s.T, q_rot[m], precision=HIGHEST, preferred_element_type=F32)
        grad_j[rows_of(m), :HD] = turned(d_q, cosine, -sine).astype(BF16)
        grad_j[rows_of(m), HD:2 * HD] = turned(d_k, cosine, -sine).astype(BF16)
        grad_j[rows_of(m), 2 * HD:] = d_val.astype(BF16)

    chunks = width // 512

    def outward(m):
        def body(i, c):
            r = pl.ds(pl.multiple_of(i * 512, 512), 512)
            part[m, :, r] = dot_nt(ctx[rows_of(m), :], w[r, 3 * HD:]).astype(BF16)
            return c

        lax.fori_loop(0, chunks, body, 0)

    def widen_o():
        def body(i, c):
            r = pl.ds(pl.multiple_of(i * 512, 512), 512)
            grad[r, 3 * HD:] = dot(cot_t[r, :], ctx[...])
            return c

        lax.fori_loop(0, chunks, body, 0)

    def widen_q():
        def body(i, c):
            r = pl.ds(pl.multiple_of(i * 512, 512), 512)
            grad[r, :3 * HD] = dot(tok_t[r, :], grad_j[...])
            return c

        lax.fori_loop(0, chunks, body, 0)

    def retract():
        for m in (0, 1):
            back[rows_of(m), :] = dot(cot[m], w[:, 3 * HD:]).astype(BF16)

    def rs_y(way, d, j):
        return remote(
            sq.at[way, d - 1, j], rq.at[way, d - 1, j], rs_ss.at[way, d - 1, j], rs_rs.at[way, d - 1, j],
            up if way == 0 else down,
        )

    def rs_step(j, u):
        d = 4 - u
        for way in (0, 1):
            if d == 4 and not long(way, j):
                continue
            sign = 1 if way == 0 else -1
            own = grad[row_at((zh - j + NZ) % NZ, (y + sign * d + NY) % NY), :]
            if d < 3 or (d == 3 and long(way, j)):
                rs_y(way, d + 1, j).wait_recv()
                own = own + rq[way, d, j].astype(F32)
            sq[way, d - 1, j] = own.astype(BF16)
            rs_y(way, d, j).start()

    def rs_here(j):
        for way in (0, 1):
            rs_y(way, 1, j).wait_recv()
        own = grad[row_at((zh - j + NZ) % NZ, y), :]
        return own + rq[0, 0, j].astype(F32) + rq[1, 0, j].astype(F32)

    def rs_z(j):
        return remote(zs.at[j], zr.at[j], rsz_ss.at[j], rsz_rs.at[j], at_z(NZ - j))

    def rs_out(j):
        zs[j] = rs_here(j).astype(BF16)
        rs_z(j).start()

    def rs_end():
        total = rs_here(0)
        for j in (1, 2, 3):
            rs_z(j).wait_recv()
        total = total + zr[2].astype(F32)
        across = zr[1].astype(F32) + zr[3].astype(F32)
        for at, value in ((pick, total), (1 - pick, across)):
            cols = pl.ds(pl.multiple_of(at * HD, HD), HD)
            for c in range(3):
                gq_out[c, :, cols] = value[:, c * HD:(c + 1) * HD]
            go_out[:, cols] = value[:, 3 * HD:]

    def rs_drain():
        for j in range(NZ):
            if j > 0:
                rs_z(j).wait_send()
            for way in (0, 1):
                for d in (1, 2, 3, 4):
                    if d < 4 or long(way, j):
                        rs_y(way, d, j).wait_send()

    def mx_core(m):
        return remote(part.at[m, place(1 - core), :], part_c.at[m], mx_ss.at[m, 0], mx_rs.at[m, 0], core_peer)

    def mx_x(m, k):
        away = pl.ds(pl.multiple_of(((x + k) % NX) * quarter, 16), quarter)
        return remote(sum_c.at[m, away, :], recv_x.at[m, k - 1], mx_ss.at[m, k], mx_rs.at[m, k], at_x(k))

    def mx_z(i):
        m, peer = ((0, lo_peer), (1, partner), (1, partner_lo))[i]
        at = pl.ds(pl.multiple_of((lo if i == 1 else 1 - lo) * eighth, 16), eighth)
        return remote(sum_x.at[m, at, :], recv_z.at[i], mx_ss.at[0, 4 + i], mx_rs.at[0, 4 + i], peer)

    def back_copy(stage, got=False):
        if stage == 0:
            at, peer = place(core, x, 1 - lo if got else lo), lo_peer
        elif stage == 4:
            at, peer = place(1 - core if got else core), core_peer
        else:
            at, peer = place(core, (x - stage + NX) % NX if got else x), at_x(stage)
        return remote(mixed.at[at, :], mixed.at[at, :], mx_ss.at[1, 4 + stage], mx_rs.at[1, 4 + stage], peer)

    def stage_x(m):
        mx_core(m).wait_recv()

        def body(i, c):
            r = pl.ds(pl.multiple_of(i * 16, 16), 16)
            there = pl.ds(pl.multiple_of(core * half + i * 16, 16), 16)
            sum_c[m, r, :] = (part[m, there, :].astype(F32) + part_c[m, r, :].astype(F32)).astype(BF16)
            return c

        lax.fori_loop(0, half // 16, body, 0)
        for k in (1, 3, 2):
            mx_x(m, k).start()

    def stage_z(m):
        total = sum_c[m, pl.ds(pl.multiple_of(x * quarter, 16), quarter), :].astype(F32)
        for k in (1, 3, 2):
            mx_x(m, k).wait_recv()
            total = total + recv_x[m, k - 1].astype(F32)
        sum_x[m] = total.astype(BF16)
        for i in ((0,), (1, 2))[m]:
            mx_z(i).start()

    def stage_back():
        total = sum_x[0, pl.ds(pl.multiple_of(lo * eighth, 16), eighth), :].astype(F32)
        for i in range(3):
            mx_z(i).wait_recv()
            total = total + recv_z[i].astype(F32)
        at = place(core, x, lo)
        mixed[at, :] = (tok[0, at, :].astype(F32) + total).astype(BF16)
        back_copy(0).start()

    def stage_back_x():
        back_copy(0, True).wait_recv()
        for k in (1, 3, 2):
            back_copy(k).start()

    def stage_back_core():
        for k in (1, 3, 2):
            back_copy(k, True).wait_recv()
        back_copy(4).start()

    def mx_drain():
        for m in (0, 1):
            mx_core(m).wait_send()
            for k in (1, 2, 3):
                mx_x(m, k).wait_send()
        for i in range(3):
            mx_z(i).wait_send()
        for stage in range(5):
            back_copy(stage).wait_send()

    def leave(got):
        at = place(1 - core if got else core)
        return pltpu.make_async_copy(mixed.at[at, :], mixed_out.at[at, :], load_sem.at[got])

    tk_copy(0, 0).start()
    ag_step(0, 0)
    ag_z(1).start()
    ag_z(3).start()
    tk_copy(1, 0).start()
    doc_copy().start()
    ag_z(2).start()
    flip(tok, tok_t, 0)
    ag_step(0, 1)
    tk_lo(0)
    ag_step(1, 0)
    ag_step(3, 0)
    flip(cot, cot_t, 0)
    ag_step(0, 2)
    ag_step(1, 1)
    tk_x(0)
    tk_lo(1)
    ag_step(2, 0)
    ag_step(3, 1)
    ag_step(0, 3)
    ag_step(1, 2)
    tk_x(1)
    ag_step(2, 1)
    ag_step(3, 2)
    ag_step(1, 3)
    tk_core(0)
    ag_step(2, 2)
    ag_step(3, 3)
    ag_step(2, 3)
    tk_end(0)
    flip(tok, tok_t, 1)
    ag_end()

    project(0)
    attend(0)
    tk_core(1)
    outward(0)
    mx_core(0).start()
    project(1)
    doc_copy().wait_recv()
    attend(1)
    outward(1)
    mx_core(1).start()
    tk_end(1)
    stage_x(0)
    flip(cot, cot_t, 1)
    stage_x(1)
    retract()
    retreat(0)
    retreat(1)
    stage_z(0)
    widen_o()
    widen_q()
    rs_step(2, 0)
    rs_step(1, 0)
    stage_z(1)
    rs_step(2, 1)
    rs_step(3, 0)
    rs_step(1, 1)
    rs_step(2, 2)
    rs_step(0, 0)
    rs_step(3, 1)
    stage_back()
    rs_step(1, 2)
    rs_step(2, 3)
    rs_step(0, 1)
    stage_back_x()
    rs_step(3, 2)
    rs_out(2)
    rs_step(1, 3)
    rs_step(0, 2)
    rs_step(3, 3)
    rs_out(1)
    rs_step(0, 3)
    rs_out(3)
    stage_back_core()
    leave(0).start()
    rs_end()
    back_copy(4, True).wait_recv()
    leave(1).start()

    ag_drain()
    tk_drain()
    doc_copy().wait_send()
    rs_drain()
    mx_drain()
    leave(0).wait()
    leave(1).wait()


def local(tokens, doc_ids, qkv_weight, out_weight, cotangent):
    length, width = tokens.shape
    rows, _, feature = qkv_weight.shape
    block = 4 * HD
    frequency = 10000.0 ** (-2.0 * np.arange(HD // 2) / HD)
    angles = np.arange(length)[:, None] * frequency[None, :]
    cosine = jnp.asarray(np.concatenate([np.cos(angles), np.cos(angles)], axis=1), F32)
    sine = jnp.asarray(np.concatenate([-np.sin(angles), np.sin(angles)], axis=1), F32)
    vmem = pl.BlockSpec(memory_space=pltpu.VMEM)
    hbm = pl.BlockSpec(memory_space=pl.ANY)
    dma = pltpu.SemaphoreType.DMA
    half = length // NC
    quarter = half // NX
    mixed, grad_q, grad_o = pl.pallas_call(
        kernel,
        out_shape=(
            jax.ShapeDtypeStruct((length, width), BF16),
            jax.ShapeDtypeStruct((3, rows, feature), F32),
            jax.ShapeDtypeStruct((rows, feature), F32),
        ),
        in_specs=[hbm, hbm] + [vmem] * 5,
        out_specs=(hbm, vmem, vmem),
        scratch_shapes=[
            pltpu.VMEM((2, length, width), BF16),
            pltpu.VMEM((2, length, width), BF16),
            pltpu.VMEM((width, 2 * length), BF16),
            pltpu.VMEM((width, 2 * length), BF16),
            pltpu.VMEM((2, 8, length), jnp.int32),
            pltpu.VMEM((2, rows, block), BF16),
            pltpu.VMEM((width, block), BF16),
            pltpu.VMEM((2 * length, 3 * HD), BF16),
            pltpu.VMEM((2 * length, HD), BF16),
            pltpu.VMEM((2 * length, HD), BF16),
            pltpu.VMEM((2, length, length), F32),
            pltpu.VMEM((2, length, HD), F32),
            pltpu.VMEM((2, length, HD), F32),
            pltpu.VMEM((2 * length, 3 * HD), BF16),
            pltpu.VMEM((width, block), F32),
            pltpu.VMEM((2, 4, NZ, rows, block), BF16),
            pltpu.VMEM((2, 4, NZ, rows, block), BF16),
            pltpu.VMEM((NZ, rows, block), BF16),
            pltpu.VMEM((NZ, rows, block), BF16),
            pltpu.VMEM((2, length, width), BF16),
            pltpu.VMEM((2, half, width), BF16),
            pltpu.VMEM((2, half, width), BF16),
            pltpu.VMEM((2, NX - 1, quarter, width), BF16),
            pltpu.VMEM((2, quarter, width), BF16),
            pltpu.VMEM((3, quarter // NL, width), BF16),
            pltpu.VMEM((length, width), BF16),
            dma((2,)),
            dma((2, 4, NZ)),
            dma((2, 4, NZ)),
            dma((NZ,)),
            dma((NZ,)),
            dma((2, 4, NZ)),
            dma((2, 4, NZ)),
            dma((NZ,)),
            dma((NZ,)),
            dma((2, 7)),
            dma((2, 7)),
            dma((2, 9)),
            dma((2, 9)),
        ],
        compiler_params=pltpu.CompilerParams(
            collective_id=0, has_side_effects=True, vmem_limit_bytes=56 * 1024 * 1024
        ),
        name="layer",
    )(
        tokens,
        cotangent,
        qkv_weight.transpose(1, 0, 2),
        out_weight.T,
        doc_ids.reshape(1, length),
        cosine,
        sine,
    )
    return mixed, grad_q.transpose(1, 0, 2), grad_o.T


def solution(mesh):
    placed = (
        P("blk", None),
        P("blk"),
        P("blk", None, "tensor"),
        P("tensor", "blk"),
        P("blk", None),
    )
    return jax.shard_map(
        local,
        mesh=mesh,
        in_specs=placed,
        out_specs=(P("blk", None), P("blk", None, "tensor"), P("tensor", "blk")),
        check_vma=False,
    )
```

time: 720 us -> 112 us (0.16)
  the two profiles are of different devices: /device:TPU:6 before, /device:TPU:64 now
where the time goes in v3:
time: 112 us
  Pallas kernels  107 us (96%)
  local copies, waits for them, and re-layouts  3.84 us (3%)
    pallas_call x1, Pallas kernels, local(): pl.pallas_call(kernel, out_shape=(jax.ShapeDtypeStruct((length, width), B...  107 us
    unnamed x7, local copies, waits for them, and re-layouts  3.84 us

profile of v3, /device:TPU:64, one launch (start us, length us, event | category | flops | bytes accessed | tf_op | source)
XLA Modules:
  0.0 111.6 jit_solution(7687049108484165213)
XLA Ops:
  0.6 107.1 %layer.1 = (bf16[256,2560]{1,0:T(8,128)(2,1)}, f32[3,80,256]{2,1,0:T(8,128)}, f32[80,256]{1,0:T(8,128)}) custom-call(bf16[256,2560]{1,0:T(8,128)(2,1)} %tokens_hbm.1, bf16[256,2560]{1,0:T(8,128)(2,1)} %cot_hbm.1, bf16[3,80,256]{2,1,0:T(8,128)(2,1)} %bitcast.6, bf16[80,256]{1,0:T(8,128)(2,1)} %bitcast.8, s32[1,256]{1,0:T(1,128)} %bitcast.9, ...), custom_call_target="tpu_custom_call" | custom-call | tf_op jit(solution)/shard_map/layer/pallas_call | solution.py:498
  107.8 0.0 copy-start
  107.8 0.0 copy-start.1
  107.8 2.5 %copy.13 = bf16[256,2560]{1,0:T(8,128)(2,1)} copy(bf16[256,2560]{1,0:T(8,128)(2,1)} %get-tuple-element.12) | data formatting | bytes 2621440
  110.3 0.0 copy-done
  110.3 0.7 copy.14
  111.0 0.0 copy-done.1
  111.0 0.6 copy.15
Async XLA Ops:
  107.8 2.5 %copy-start = (f32[3,80,256]{2,1,0:T(8,128)S(1)}, f32[3,80,256]{2,1,0:T(8,128)}, u32[]{:S(2)}) copy-start(f32[3,80,256]{2,1,0:T(8,128)} %get-tuple-element.7) | copy-start | bytes 737284
  107.8 3.2 %copy-start.1 = (f32[80,256]{1,0:T(8,128)S(1)}, f32[80,256]{1,0:T(8,128)}, u32[]{:S(2)}) copy-start(f32[80,256]{1,0:T(8,128)} %get-tuple-element.8) | copy-start | bytes 245764

commit v4 on v3

--- a/solution.py
+++ b/solution.py
@@ -35,7 +35,7 @@
     tokens_hbm, cot_hbm, wq_in, wo_in, doc_in, cos_in, sin_in,
     mixed_out, gq_out, go_out,
     tok, cot, tok_t, cot_t, docs, staged, w, joined, ctx, back, probs, q_rot, k_rot, grad_j,
-    grad, sq, rq, zs, zr, part, part_c, sum_c, recv_x, sum_x, recv_z, mixed,
+    sq, rq, zs, zr, part, part_c, sum_c, recv_x, sum_x, recv_z, mixed,
     load_sem, ag_ss, ag_rs, agz_ss, agz_rs, rs_ss, rs_rs, rsz_ss, rsz_rs, tk_ss, tk_rs, mx_ss, mx_rs,
 ):
     blk = lax.axis_index("blk")
@@ -243,21 +243,9 @@
 
         lax.fori_loop(0, chunks, body, 0)
 
-    def widen_o():
-        def body(i, c):
-            r = pl.ds(pl.multiple_of(i * 512, 512), 512)
-            grad[r, 3 * HD:] = dot(cot_t[r, :], ctx[...])
-            return c
-
-        lax.fori_loop(0, chunks, body, 0)
-
-    def widen_q():
-        def body(i, c):
-            r = pl.ds(pl.multiple_of(i * 512, 512), 512)
-            grad[r, :3 * HD] = dot(tok_t[r, :], grad_j[...])
-            return c
-
-        lax.fori_loop(0, chunks, body, 0)
+    def block_grad(z, yy):
+        r = row_at(z, yy)
+        return jnp.concatenate([dot(tok_t[r, :], grad_j[...]), dot(cot_t[r, :], ctx[...])], axis=1)
 
     def retract():
         for m in (0, 1):
@@ -275,7 +263,7 @@
             if d == 4 and not long(way, j):
                 continue
             sign = 1 if way == 0 else -1
-            own = grad[row_at((zh - j + NZ) % NZ, (y + sign * d + NY) % NY), :]
+            own = block_grad((zh - j + NZ) % NZ, (y + sign * d + NY) % NY)
             if d < 3 or (d == 3 and long(way, j)):
                 rs_y(way, d + 1, j).wait_recv()
                 own = own + rq[way, d, j].astype(F32)
@@ -283,9 +271,9 @@
             rs_y(way, d, j).start()
 
     def rs_here(j):
+        own = block_grad((zh - j + NZ) % NZ, y)
         for way in (0, 1):
             rs_y(way, 1, j).wait_recv()
-        own = grad[row_at((zh - j + NZ) % NZ, y), :]
         return own + rq[0, 0, j].astype(F32) + rq[1, 0, j].astype(F32)
 
     def rs_z(j):
@@ -392,86 +380,84 @@
         at = place(1 - core if got else core)
         return pltpu.make_async_copy(mixed.at[at, :], mixed_out.at[at, :], load_sem.at[got])
 
-    tk_copy(0, 0).start()
     ag_step(0, 0)
     ag_z(1).start()
     ag_z(3).start()
+    tk_copy(0, 0).start()
+    ag_z(2).start()
     tk_copy(1, 0).start()
     doc_copy().start()
-    ag_z(2).start()
     flip(tok, tok_t, 0)
     ag_step(0, 1)
-    tk_lo(0)
+    flip(cot, cot_t, 0)
     ag_step(1, 0)
     ag_step(3, 0)
-    flip(cot, cot_t, 0)
+    tk_lo(0)
     ag_step(0, 2)
     ag_step(1, 1)
+    ag_step(2, 0)
+    tk_lo(1)
+    ag_step(3, 1)
     tk_x(0)
-    tk_lo(1)
-    ag_step(2, 0)
-    ag_step(3, 1)
     ag_step(0, 3)
     ag_step(1, 2)
+    ag_step(2, 1)
     tk_x(1)
-    ag_step(2, 1)
     ag_step(3, 2)
     ag_step(1, 3)
-    tk_core(0)
     ag_step(2, 2)
     ag_step(3, 3)
     ag_step(2, 3)
-    tk_end(0)
-    flip(tok, tok_t, 1)
+    tk_core(0)
     ag_end()
 
     project(0)
     attend(0)
-    tk_core(1)
-    outward(0)
-    mx_core(0).start()
+    tk_end(0)
     project(1)
     doc_copy().wait_recv()
     attend(1)
     outward(1)
     mx_core(1).start()
+    tk_core(1)
+    outward(0)
+    mx_core(0).start()
+    flip(tok, tok_t, 1)
+    stage_x(1)
     tk_end(1)
     stage_x(0)
     flip(cot, cot_t, 1)
-    stage_x(1)
     retract()
     retreat(0)
     retreat(1)
-    stage_z(0)
-    widen_o()
-    widen_q()
+    stage_z(1)
     rs_step(2, 0)
     rs_step(1, 0)
-    stage_z(1)
+    rs_step(3, 0)
     rs_step(2, 1)
-    rs_step(3, 0)
     rs_step(1, 1)
+    stage_z(0)
+    rs_step(3, 1)
     rs_step(2, 2)
+    rs_step(1, 2)
     rs_step(0, 0)
-    rs_step(3, 1)
+    rs_step(3, 2)
     stage_back()
-    rs_step(1, 2)
     rs_step(2, 3)
+    rs_step(1, 3)
     rs_step(0, 1)
+    rs_out(2)
     stage_back_x()
-    rs_step(3, 2)
-    rs_out(2)
-    rs_step(1, 3)
-    rs_step(0, 2)
     rs_step(3, 3)
     rs_out(1)
-    rs_step(0, 3)
+    rs_step(0, 2)
     rs_out(3)
     stage_back_core()
     leave(0).start()
-    rs_end()
+    rs_step(0, 3)
     back_copy(4, True).wait_recv()
     leave(1).start()
+    rs_end()
 
     ag_drain()
     tk_drain()
@@ -480,6 +466,31 @@
     mx_drain()
     leave(0).wait()
     leave(1).wait()
+
+
+def settle(*refs):
+    ins, outs, held, sems = refs[:3], refs[3:6], refs[6:9], refs[9]
+    parts = []
+    for a in range(3):
+        n = ins[a].shape[0]
+        cut = n // 4 if a == 0 else n
+        for at in range(0, n, cut):
+            parts.append((a, pl.ds(at, cut)))
+    loads = [
+        pltpu.make_async_copy(ins[a].at[at], held[a].at[at], sems.at[0, i])
+        for i, (a, at) in enumerate(parts)
+    ]
+    stores = [
+        pltpu.make_async_copy(held[a].at[at], outs[a].at[at], sems.at[1, i])
+        for i, (a, at) in enumerate(parts)
+    ]
+    for load in loads:
+        load.start()
+    for load, store in zip(loads, stores):
+        load.wait()
+        store.start()
+    for store in stores:
+        store.wait()
 
 
 def local(tokens, doc_ids, qkv_weight, out_weight, cotangent):
@@ -519,7 +530,6 @@
             pltpu.VMEM((2, length, HD), F32),
             pltpu.VMEM((2, length, HD), F32),
             pltpu.VMEM((2 * length, 3 * HD), BF16),
-            pltpu.VMEM((width, block), F32),
             pltpu.VMEM((2, 4, NZ, rows, block), BF16),
             pltpu.VMEM((2, 4, NZ, rows, block), BF16),
             pltpu.VMEM((NZ, rows, block), BF16),
@@ -558,6 +568,15 @@
         cosine,
         sine,
     )
+    outs = (mixed, grad_q, grad_o)
+    mixed, grad_q, grad_o = pl.pallas_call(
+        settle,
+        out_shape=tuple(jax.ShapeDtypeStruct(o.shape, o.dtype) for o in outs),
+        in_specs=[hbm] * 3,
+        out_specs=(hbm,) * 3,
+        scratch_shapes=[pltpu.VMEM(o.shape, o.dtype) for o in outs] + [dma((2, 6))],
+        name="settle",
+    )(*outs)
     return mixed, grad_q.transpose(1, 0, 2), grad_o.T
 
 

time: 112 us -> 106 us (0.946)
  the two profiles are of different devices: /device:TPU:64 before, /device:TPU:6 now
where the time goes in v4:
time: 106 us
  Pallas kernels  105 us (99%)
    pallas_call x1, Pallas kernels, local(): pl.pallas_call(kernel, out_shape=(jax.ShapeDtypeStruct((length, width), B...  103 us
    pallas_call x1, Pallas kernels, local(): pl.pallas_call(settle, out_shape=tuple((jax.ShapeDtypeStruct(o.shape, o.d...  2.23 us

profile of v4, /device:TPU:6, one launch (start us, length us, event | category | flops | bytes accessed | tf_op | source)
XLA Modules:
  0.0 105.9 jit_solution(16704661104004188397)
XLA Ops:
  0.6 102.9 %layer.1 = (bf16[256,2560]{1,0:T(8,128)(2,1)}, f32[3,80,256]{2,1,0:T(8,128)}, f32[80,256]{1,0:T(8,128)}) custom-call(bf16[256,2560]{1,0:T(8,128)(2,1)} %tokens_hbm.1, bf16[256,2560]{1,0:T(8,128)(2,1)} %cot_hbm.1, bf16[3,80,256]{2,1,0:T(8,128)(2,1)} %bitcast.5, bf16[80,256]{1,0:T(8,128)(2,1)} %bitcast.6, s32[1,256]{1,0:T(1,128)} %bitcast.7, ...), custom_call_target="tpu_custom_call" | custom-call | tf_op jit(solution)/shard_map/layer/pallas_call | solution.py:509
  103.5 2.2 %settle.1 = (bf16[256,2560]{1,0:T(8,128)(2,1)}, f32[3,80,256]{2,1,0:T(8,128)}, f32[80,256]{1,0:T(8,128)}) custom-call(bf16[256,2560]{1,0:T(8,128)(2,1)} %get-tuple-element.9.refs_0_, f32[3,80,256]{2,1,0:T(8,128)} %get-tuple-element.10.refs_1_, f32[80,256]{1,0:T(8,128)} %get-tuple-element.11.refs_2_), custom_call_target="tpu_custom_call" | custom-call | tf_op jit(solution)/shard_map/settle/pallas_call | solution.py:572

commit v5 on v4

--- a/solution.py
+++ b/solution.py
@@ -322,7 +322,8 @@
         elif stage == 4:
             at, peer = place(1 - core if got else core), core_peer
         else:
-            at, peer = place(core, (x - stage + NX) % NX if got else x), at_x(stage)
+            k, ll = (stage, lo) if stage < 4 else (stage - 4, 1 - lo)
+            at, peer = place(core, (x - k + NX) % NX if got else x, ll), at_x(k)
         return remote(mixed.at[at, :], mixed.at[at, :], mx_ss.at[1, 4 + stage], mx_rs.at[1, 4 + stage], peer)
 
     def stage_x(m):
@@ -354,16 +355,18 @@
             total = total + recv_z[i].astype(F32)
         at = place(core, x, lo)
         mixed[at, :] = (tok[0, at, :].astype(F32) + total).astype(BF16)
-        back_copy(0).start()
+        for stage in (0, 1, 3, 2):
+            back_copy(stage).start()
 
     def stage_back_x():
         back_copy(0, True).wait_recv()
         for k in (1, 3, 2):
-            back_copy(k).start()
+            back_copy(4 + k).start()
 
     def stage_back_core():
         for k in (1, 3, 2):
             back_copy(k, True).wait_recv()
+            back_copy(4 + k, True).wait_recv()
         back_copy(4).start()
 
     def mx_drain():
@@ -373,7 +376,7 @@
                 mx_x(m, k).wait_send()
         for i in range(3):
             mx_z(i).wait_send()
-        for stage in range(5):
+        for stage in range(8):
             back_copy(stage).wait_send()
 
     def leave(got):
@@ -552,8 +555,8 @@
             dma((NZ,)),
             dma((2, 7)),
             dma((2, 7)),
-            dma((2, 9)),
-            dma((2, 9)),
+            dma((2, 12)),
+            dma((2, 12)),
         ],
         compiler_params=pltpu.CompilerParams(
             collective_id=0, has_side_effects=True, vmem_limit_bytes=56 * 1024 * 1024

time: 106 us -> 105 us (level)
    pallas_call x1, Pallas kernels: 103 us -> 101 us  [local(): pl.pallas_call(kernel, out_shape=(jax.ShapeDtypeStruct((length, width), B...]
where the time goes in v5:
time: 105 us; the launch traced here: 104 us
  Pallas kernels  104 us (99%)
    pallas_call x1, Pallas kernels, local(): pl.pallas_call(kernel, out_shape=(jax.ShapeDtypeStruct((length, width), B...  101 us
    pallas_call x1, Pallas kernels, local(): pl.pallas_call(settle, out_shape=tuple((jax.ShapeDtypeStruct(o.shape, o.d...  2.23 us

profile of v5, /device:TPU:6, one launch (start us, length us, event | category | flops | bytes accessed | tf_op | source)
XLA Modules:
  0.0 104.3 jit_solution(17897307108316892807)
XLA Ops:
  0.6 101.3 %layer.1 = (bf16[256,2560]{1,0:T(8,128)(2,1)}, f32[3,80,256]{2,1,0:T(8,128)}, f32[80,256]{1,0:T(8,128)}) custom-call(bf16[256,2560]{1,0:T(8,128)(2,1)} %tokens_hbm.1, bf16[256,2560]{1,0:T(8,128)(2,1)} %cot_hbm.1, bf16[3,80,256]{2,1,0:T(8,128)(2,1)} %bitcast.5, bf16[80,256]{1,0:T(8,128)(2,1)} %bitcast.6, s32[1,256]{1,0:T(1,128)} %bitcast.7, ...), custom_call_target="tpu_custom_call" | custom-call | tf_op jit(solution)/shard_map/layer/pallas_call | solution.py:512
  101.9 2.2 %settle.1 = (bf16[256,2560]{1,0:T(8,128)(2,1)}, f32[3,80,256]{2,1,0:T(8,128)}, f32[80,256]{1,0:T(8,128)}) custom-call(bf16[256,2560]{1,0:T(8,128)(2,1)} %get-tuple-element.9.refs_0_, f32[3,80,256]{2,1,0:T(8,128)} %get-tuple-element.10.refs_1_, f32[80,256]{1,0:T(8,128)} %get-tuple-element.11.refs_2_), custom_call_target="tpu_custom_call" | custom-call | tf_op jit(solution)/shard_map/settle/pallas_call | solution.py:575
